TPU v7x, 256 devices: a whole 4x4x8 slice. The times are simulated.
256 devices in a mesh: dom: 16 (over y, x), panel: 16 (over z, core).
Axes of the slice: x: 4, y: 4, z: 8, core: 2. Of those that a mesh axis runs over, the one named last changes fastest.
Arguments:
- start_block: float32 [256, 16384], P('panel', 'dom'), may hold values from -1500 to 1500
- prior_dirs: float32 [256, 16384], P('panel', 'dom'), may hold values from -6 to 6
- degree: float32 [16384], P('dom'), may hold values from 1 to 4
- tiles: float32 [512, 128, 128], P('dom'), may hold values from -0.21875 to 0.21875
- tile_rows: int32 [512], P('dom'), may hold values from 0 to 7
- tile_cols: int32 [512], P('dom'), may hold values from 0 to 7
- cut_rows: int32 [4096], P('dom'), may hold values from 0 to 1023
- cut_count: int32 [16], P('dom'), may hold values from 128 to 256, as said below
- bound_tiles: float32 [256, 128, 128], P('dom'), may hold values from -0.21875 to 0.21875
- bound_rows: int32 [256], P('dom'), may hold values from 0 to 7
- bound_cols: int32 [256], P('dom'), may hold values from 0 to 31
- rot_xx: float32 [256, 256], replicated, may hold values from -0.21875 to 0.21875
- rot_xr: float32 [256, 256], replicated, may hold values from -0.21875 to 0.21875
- rot_xp: float32 [256, 256], replicated, may hold values from -0.21875 to 0.21875
- rot_pr: float32 [256, 256], replicated, may hold values from -0.25 to 0.25
- rot_pp: float32 [256, 256], replicated, may hold values from -0.25 to 0.25
Outputs:
- block: float32 [256, 16384], P('panel', 'dom')
- directions: float32 [256, 16384], P('panel', 'dom')
- ritz: float32 [256], P('panel')
Inputs may be any that keep to these rules, and one draw needn't show every extreme that they name: `cut_count`: at most 256 live entries in a group's cut list; in every draw some group has exactly 256.
All inputs are finite; a program needn't handle non-finite values.
Results may differ from a plain program's by a relative error of at most 0.0003.
Values sent between devices are 32-bit elements; how exact they have to be, the bound alone decides.
A program may use at most 64 MiB of HBM per device.

v0:
```python
import jax
import jax.numpy as jnp
from jax import lax
from jax.sharding import PartitionSpec as P

ITERS = 4


def tile_product(source, tile_set, row_ids, col_ids, blocks_out):
    width = source.shape[0]
    tile = tile_set.shape[1]
    blocks = source.reshape(width, -1, tile)
    picked = jnp.take(blocks, col_ids, axis=1)
    product = jnp.einsum("mtk,tjk->mtj", picked, tile_set, precision=lax.Precision.HIGHEST)
    onehot = (row_ids[:, None] == jnp.arange(blocks_out, dtype=jnp.int32)[None, :]).astype(
        jnp.float32
    )
    summed = jnp.einsum("mtj,tr->mrj", product, onehot, precision=lax.Precision.HIGHEST)
    return summed.reshape(width, blocks_out * tile)


def matmul(left, right):
    return jnp.dot(left, right, precision=lax.Precision.HIGHEST)


def local(
    start_block,
    prior_dirs,
    degree,
    tiles,
    tile_rows,
    tile_cols,
    cut_rows,
    cut_count,
    bound_tiles,
    bound_rows,
    bound_cols,
    rot_xx,
    rot_xr,
    rot_xp,
    rot_pr,
    rot_pp,
):
    width, ndev = start_block.shape
    nodes = ndev * lax.axis_size("dom")
    blocks_out = ndev // tiles.shape[1]
    offset = lax.axis_index("panel") * width
    live = (jnp.arange(cut_rows.shape[0], dtype=jnp.int32) < cut_count[0]).astype(jnp.float32)

    def factor(sumsq):
        return jnp.sqrt(sumsq / nodes + 1e-06)[:, None]

    directions = prior_dirs
    ritz = jnp.zeros((width,), jnp.float32)
    sumsq = lax.psum(jnp.sum(start_block * start_block, axis=1), "dom")
    block = start_block / factor(sumsq)
    for step in range(ITERS):
        outgoing = jnp.take(block, cut_rows, axis=1) * live[None, :]
        far = lax.all_gather(outgoing, "dom", axis=1, tiled=True)
        near = tile_product(block, tiles, tile_rows, tile_cols, blocks_out)
        across = tile_product(far, bound_tiles, bound_rows, bound_cols, blocks_out)
        image = degree[None, :] * block - (near + across)
        selfdot, crossdot = lax.psum(
            (jnp.sum(block * block, axis=1), jnp.sum(block * image, axis=1)), "dom"
        )
        ritz = crossdot / selfdot
        resid = image - ritz[:, None] * block
        own_xx = lax.dynamic_slice_in_dim(rot_xx, offset, width, 0)
        own_xr = lax.dynamic_slice_in_dim(rot_xr, offset, width, 0)
        own_xp = lax.dynamic_slice_in_dim(rot_xp, offset, width, 0)
        own_pr = lax.dynamic_slice_in_dim(rot_pr, offset, width, 0)
        own_pp = lax.dynamic_slice_in_dim(rot_pp, offset, width, 0)
        block_piece = lax.all_gather(block, "panel", axis=0, tiled=True)
        resid_piece = lax.all_gather(resid, "panel", axis=0, tiled=True)
        dir_piece = lax.all_gather(directions, "panel", axis=0, tiled=True)

        def term(matrix, piece):
            return matmul(matrix, piece)

        rotated = term(own_xx, block_piece) + term(own_xr, resid_piece) + term(own_xp, dir_piece)
        turned = term(own_pr, resid_piece) + term(own_pp, dir_piece)
        rotated, directions = (rotated, turned)
        sumsq = lax.psum(jnp.sum(rotated * rotated, axis=1), "dom")
        block = rotated / factor(sumsq)
    return (block, directions, ritz)


def solution(mesh):
    return jax.shard_map(
        local,
        mesh=mesh,
        in_specs=(
            P("panel", "dom"),
            P("panel", "dom"),
            P("dom"),
            P("dom", None, None),
            P("dom"),
            P("dom"),
            P("dom"),
            P("dom"),
            P("dom", None, None),
            P("dom"),
            P("dom"),
            P(),
            P(),
            P(),
            P(),
            P(),
        ),
        out_specs=(P("panel", "dom"), P("panel", "dom"), P("panel")),
        check_vma=False,
    )
```

profile of v0, /device:TPU:1, one launch (start us, length us, event | category | flops | bytes accessed | tf_op | source)
XLA Modules:
  0.0 841.0 jit_solution(16090860682599106034)
XLA Ops:
  8.3 34.2 %psum.91 = f32[16]{0:T(128)S(1)} all-reduce(f32[16]{0:T(128)S(1)} %multiply_reduce_fusion.12), channel_id=1, replica_groups=mesh['dom'=16,'panel'=16] {'dom'}, use_global_device_ids=true, to_apply=%region_1.0 | all-reduce | flops 16 | bytes 128 | tf_op jit(solution)/shard_map/psum | solution.py:55
  50.4 22.1 %all_gather.49 = f32[16,4096]{0,1:T(8,128)} all-gather(f32[16,256]{0,1:T(8,128)S(1)} %bitcast_multiply_fusion.3), channel_id=1, replica_groups=mesh['dom'=16,'panel'=16] {'dom'}, dimensions={1}, use_global_device_ids=true | all-gather | bytes 278528 | tf_op jit(solution)/shard_map/all_gather | solution.py:59
  73.2 3.2 gather_fusion.2
  76.5 3.4 fusion.34
  82.5 30.6 %all-reduce.3 = (f32[16]{0:T(128)S(1)}, f32[16]{0:T(128)S(1)}) all-reduce(f32[16]{0:T(128)S(1)} %get-tuple-element.13, f32[16]{0:T(128)S(1)} %get-tuple-element.12), channel_id=1, replica_groups=mesh['dom'=16,'panel'=16] {'dom'}, use_global_device_ids=true, to_apply=%region_3.0 | all-reduce | flops 32 | bytes 256 | tf_op jit(solution)/shard_map/psum | solution.py:63
  114.6 1.9 fusion.86
  116.5 52.8 %all-gather.15.cloned.1.call-done = f32[256,1024]{1,0:T(8,128)} async-done(((f32[16,1024]{1,0:T(8,128)}), f32[256,1024]{1,0:T(8,128)}) %all-gather.15.cloned.1.call-update) | async-done | bytes 1048592 | tf_op jit(solution)/shard_map/all_gather | solution.py:74
  171.1 37.3 %all-gather.17.cloned.1.call-done = f32[256,1024]{1,0:T(8,128)} async-done(((f32[16,1024]{1,0:T(8,128)}), f32[256,1024]{1,0:T(8,128)}) %all-gather.17.cloned.1.call-update) | async-done | bytes 1048592 | tf_op jit(solution)/shard_map/all_gather | solution.py:75
  208.4 2.0 multiply_reduce_fusion.9
  210.3 33.2 %psum.94 = f32[16]{0:T(128)S(1)} all-reduce(f32[16]{0:T(128)S(1)} %get-tuple-element.22), channel_id=1, replica_groups=mesh['dom'=16,'panel'=16] {'dom'}, use_global_device_ids=true, to_apply=%region_7.11 | all-reduce | flops 16 | bytes 128 | tf_op jit(solution)/shard_map/psum | solution.py:83
  247.0 2.4 gather_fusion.4
  250.4 21.9 %all_gather.53 = f32[16,4096]{0,1:T(8,128)} all-gather(f32[16,256]{0,1:T(8,128)S(1)} %bitcast_multiply_fusion.2), channel_id=1, replica_groups=mesh['dom'=16,'panel'=16] {'dom'}, dimensions={1}, use_global_device_ids=true | all-gather | bytes 278528 | tf_op jit(solution)/shard_map/all_gather | solution.py:59
  272.3 3.3 gather_fusion.5
  275.6 4.1 fusion.30
  282.3 31.0 %all-reduce.2 = (f32[16]{0:T(128)S(1)}, f32[16]{0:T(128)S(1)}) all-reduce(f32[16]{0:T(128)S(1)} %get-tuple-element.11, f32[16]{0:T(128)S(1)} %get-tuple-element.10), channel_id=1, replica_groups=mesh['dom'=16,'panel'=16] {'dom'}, use_global_device_ids=true, to_apply=%region_9.13 | all-reduce | flops 32 | bytes 256 | tf_op jit(solution)/shard_map/psum | solution.py:63
  314.2 1.9 fusion.70
  316.0 2.5 convolution_add_fusion.10
  318.6 1.9 fusion.84
  320.5 44.2 %all-gather.21.cloned.1.call-done = f32[256,1024]{1,0:T(8,128)} async-done(((f32[16,1024]{1,0:T(8,128)}), f32[256,1024]{1,0:T(8,128)}) %all-gather.21.cloned.1.call-update) | async-done | bytes 1048592 | tf_op jit(solution)/shard_map/all_gather | solution.py:74
  366.6 37.1 %all-gather.23.cloned.1.call-done = f32[256,1024]{1,0:T(8,128)} async-done(((f32[16,1024]{1,0:T(8,128)}), f32[256,1024]{1,0:T(8,128)}) %all-gather.23.cloned.1.call-update) | async-done | bytes 1048592 | tf_op jit(solution)/shard_map/all_gather | solution.py:75
  403.7 2.0 multiply_reduce_fusion.6
  405.6 33.2 %psum.97 = f32[16]{0:T(128)S(1)} all-reduce(f32[16]{0:T(128)S(1)} %get-tuple-element.24), channel_id=1, replica_groups=mesh['dom'=16,'panel'=16] {'dom'}, use_global_device_ids=true, to_apply=%region_13.17 | all-reduce | flops 16 | bytes 128 | tf_op jit(solution)/shard_map/psum | solution.py:83
  442.3 2.4 gather_fusion.7
  445.8 21.9 %all_gather.57 = f32[16,4096]{0,1:T(8,128)} all-gather(f32[16,256]{0,1:T(8,128)S(1)} %bitcast_multiply_fusion.1), channel_id=1, replica_groups=mesh['dom'=16,'panel'=16] {'dom'}, dimensions={1}, use_global_device_ids=true | all-gather | bytes 278528 | tf_op jit(solution)/shard_map/all_gather | solution.py:59
  467.7 3.3 gather_fusion.8
  471.0 4.1 fusion.26
  477.7 31.0 %all-reduce.1 = (f32[16]{0:T(128)S(1)}, f32[16]{0:T(128)S(1)}) all-reduce(f32[16]{0:T(128)S(1)} %get-tuple-element.9, f32[16]{0:T(128)S(1)} %get-tuple-element.8), channel_id=1, replica_groups=mesh['dom'=16,'panel'=16] {'dom'}, use_global_device_ids=true, to_apply=%region_15.19 | all-reduce | flops 32 | bytes 256 | tf_op jit(solution)/shard_map/psum | solution.py:63
  509.5 1.9 fusion.68
  511.3 2.5 convolution_add_fusion.6
  513.9 1.9 fusion.82
  515.8 44.2 %all-gather.27.cloned.1.call-done = f32[256,1024]{1,0:T(8,128)} async-done(((f32[16,1024]{1,0:T(8,128)}), f32[256,1024]{1,0:T(8,128)}) %all-gather.27.cloned.1.call-update) | async-done | bytes 1048592 | tf_op jit(solution)/shard_map/all_gather | solution.py:74
  561.8 37.3 %all-gather.29.cloned.1.call-done = f32[256,1024]{1,0:T(8,128)} async-done(((f32[16,1024]{1,0:T(8,128)}), f32[256,1024]{1,0:T(8,128)}) %all-gather.29.cloned.1.call-update) | async-done | bytes 1048592 | tf_op jit(solution)/shard_map/all_gather | solution.py:75
  599.1 2.0 multiply_reduce_fusion.3
  601.1 33.2 %psum.100 = f32[16]{0:T(128)S(1)} all-reduce(f32[16]{0:T(128)S(1)} %get-tuple-element.26), channel_id=1, replica_groups=mesh['dom'=16,'panel'=16] {'dom'}, use_global_device_ids=true, to_apply=%region_19.23 | all-reduce | flops 16 | bytes 128 | tf_op jit(solution)/shard_map/psum | solution.py:83
  637.7 2.4 gather_fusion.10
  641.2 21.9 %all_gather.61 = f32[16,4096]{0,1:T(8,128)} all-gather(f32[16,256]{0,1:T(8,128)S(1)} %bitcast_multiply_fusion), channel_id=1, replica_groups=mesh['dom'=16,'panel'=16] {'dom'}, dimensions={1}, use_global_device_ids=true | all-gather | bytes 278528 | tf_op jit(solution)/shard_map/all_gather | solution.py:59
  663.1 3.3 gather_fusion.11
  666.4 4.1 fusion.22
  673.1 31.0 %all-reduce = (f32[16]{0:T(128)S(1)}, f32[16]{0:T(128)S(1)}) all-reduce(f32[16]{0:T(128)S(1)} %get-tuple-element.7, f32[16]{0:T(128)S(1)} %get-tuple-element.6), channel_id=1, replica_groups=mesh['dom'=16,'panel'=16] {'dom'}, use_global_device_ids=true, to_apply=%region_21.25 | all-reduce | flops 32 | bytes 256 | tf_op jit(solution)/shard_map/psum | solution.py:63
  705.0 1.9 fusion.66
  706.8 2.0 convolution_add_fusion.2
  708.8 1.9 fusion.80
  710.7 44.7 %all-gather.33.cloned.1.call-done = f32[256,1024]{1,0:T(8,128)} async-done(((f32[16,1024]{1,0:T(8,128)}), f32[256,1024]{1,0:T(8,128)}) %all-gather.33.cloned.1.call-update) | async-done | bytes 1048592 | tf_op jit(solution)/shard_map/all_gather | solution.py:74
  755.4 1.9 convolution_add_fusion.3
  757.4 37.0 %all-gather.35.cloned.1.call-done = f32[256,1024]{1,0:T(8,128)} async-done(((f32[16,1024]{1,0:T(8,128)}), f32[256,1024]{1,0:T(8,128)}) %all-gather.35.cloned.1.call-update) | async-done | bytes 1048592 | tf_op jit(solution)/shard_map/all_gather | solution.py:75
  794.4 2.0 multiply_reduce_fusion
  796.4 33.2 %psum.103 = f32[16]{0:T(128)S(1)} all-reduce(f32[16]{0:T(128)S(1)} %get-tuple-element.28), channel_id=1, replica_groups=mesh['dom'=16,'panel'=16] {'dom'}, use_global_device_ids=true, to_apply=%region_25.29 | all-reduce | flops 16 | bytes 128 | tf_op jit(solution)/shard_map/psum | solution.py:83
  831.7 2.5 convolution_add_fusion
  (165 shorter events, 44.2 us)
Async XLA Ops:
  7.2 69.3 %copy-start = (f32[32,128,128]{2,1,0:T(8,128)S(1)}, f32[32,128,128]{2,1,0:T(8,128)}, u32[]{:S(2)}) copy-start(f32[32,128,128]{2,1,0:T(8,128)} %param.25) | copy-start | bytes 6291460
  7.2 107.4 %all-gather.13.cloned.1.call-start = ((), (), s32[]{:S(2)}) async-start(), calls=%async_computation | async-start | bytes 1114112 | tf_op jit(solution)/shard_map/all_gather | solution.py:73
  44.2 32.2 %copy-start.34 = (s32[32]{0:T(128)S(1)}, s32[32]{0:T(128)}, u32[]{:S(2)}) copy-start(s32[32]{0:T(128)} %param.27) | copy-start | bytes 388
  44.2 32.2 %copy-start.35 = (s32[16]{0:T(128)S(1)}, s32[16]{0:T(128)}, u32[]{:S(2)}) copy-start(s32[16]{0:T(128)} %param.32) | copy-start | bytes 196
  44.2 125.1 %all-gather.15.cloned.1.call-start = ((), (), s32[]{:S(2)}) async-start(), calls=%async_computation.1 | async-start | bytes 1114112 | tf_op jit(solution)/shard_map/all_gather | solution.py:74
  49.6 30.3 %copy-start.11 = (s32[1024]{0:T(1024)}, s32[1024]{0:T(1024)S(1)}, u32[]{:S(2)}) copy-start(s32[1024]{0:T(1024)S(1)} %pad_clamp_fusion.2) | copy-start | bytes 12292
  72.5 7.3 copy-start.12
  72.5 7.6 copy-start.1
  73.2 3.2 copy-start.10
  76.4 3.8 copy-start.6
  76.4 5.6 copy-start.32
  76.4 5.6 copy-start.20
  76.4 5.6 copy-start.16
  76.5 5.8 copy-start.4
  76.5 5.8 copy-start.9
  113.8 94.6 %all-gather.17.cloned.1.call-start = ((), (), s32[]{:S(2)}) async-start(), calls=%async_computation.2 | async-start | bytes 1114112 | tf_op jit(solution)/shard_map/all_gather | solution.py:75
  114.5 204.1 %all-gather.19.cloned.1.call-start = ((), (), s32[]{:S(2)}) async-start(), calls=%async_computation.3 | async-start | bytes 1114112 | tf_op jit(solution)/shard_map/all_gather | solution.py:73
  243.6 2.6 copy-start.26
  244.3 120.4 %all-gather.21.cloned.1.call-start = ((), (), s32[]{:S(2)}) async-start(), calls=%async_computation.4 | async-start | bytes 1114112 | tf_op jit(solution)/shard_map/all_gather | solution.py:74
  250.4 29.3 %copy-start.13 = (s32[32]{0:T(128)S(1)}, s32[32]{0:T(128)}, u32[]{:S(2)}) copy-start(s32[32]{0:T(128)} %param.26) | copy-start | bytes 388
  272.3 7.8 copy-start.21
  275.6 4.4 copy-start.7
  275.6 6.3 copy-start.17
  275.6 6.5 copy-start.27
  279.8 33.6 %copy-start.28 = (f32[16]{0:T(128)S(1)}, f32[16]{0:T(128)}, u32[]{:S(2)}) copy-start(f32[16]{0:T(128)} %copy-done.26) | copy-start | bytes 196
  314.1 89.6 %all-gather.23.cloned.1.call-start = ((), (), s32[]{:S(2)}) async-start(), calls=%async_computation.5 | async-start | bytes 1114112 | tf_op jit(solution)/shard_map/all_gather | solution.py:75
  318.5 195.4 %all-gather.25.cloned.1.call-start = ((), (), s32[]{:S(2)}) async-start(), calls=%async_computation.6 | async-start | bytes 1114112 | tf_op jit(solution)/shard_map/all_gather | solution.py:73
  438.9 2.6 copy-start.29
  439.6 120.3 %all-gather.27.cloned.1.call-start = ((), (), s32[]{:S(2)}) async-start(), calls=%async_computation.7 | async-start | bytes 1114112 | tf_op jit(solution)/shard_map/all_gather | solution.py:74
  445.7 29.3 %copy-start.14 = (s32[32]{0:T(128)S(1)}, s32[32]{0:T(128)}, u32[]{:S(2)}) copy-start(s32[32]{0:T(128)} %param.26) | copy-start | bytes 388
  467.6 7.7 copy-start.22
  470.9 4.4 copy-start.8
  470.9 6.3 copy-start.18
  471.0 6.5 copy-start.30
  475.1 33.6 %copy-start.31 = (f32[16]{0:T(128)S(1)}, f32[16]{0:T(128)}, u32[]{:S(2)}) copy-start(f32[16]{0:T(128)} %copy-done.29) | copy-start | bytes 196
  509.4 89.6 %all-gather.29.cloned.1.call-start = ((), (), s32[]{:S(2)}) async-start(), calls=%async_computation.8 | async-start | bytes 1114112 | tf_op jit(solution)/shard_map/all_gather | solution.py:75
  513.9 195.0 %all-gather.31.cloned.1.call-start = ((), (), s32[]{:S(2)}) async-start(), calls=%async_computation.9 | async-start | bytes 1114112 | tf_op jit(solution)/shard_map/all_gather | solution.py:73
  634.3 2.6 copy-start.24
  635.0 120.4 %all-gather.33.cloned.1.call-start = ((), (), s32[]{:S(2)}) async-start(), calls=%async_computation.10 | async-start | bytes 1114112 | tf_op jit(solution)/shard_map/all_gather | solution.py:74
  641.1 29.4 %copy-start.15 = (s32[32]{0:T(128)S(1)}, s32[32]{0:T(128)}, u32[]{:S(2)}) copy-start(s32[32]{0:T(128)} %param.26) | copy-start | bytes 388
  663.1 7.8 copy-start.23
  666.4 4.4 copy-start.5
  666.4 6.3 copy-start.19
  666.4 6.5 copy-start.25
  672.7 34.1 %copy-start.2 = (f32[256,1024]{1,0:T(8,128)S(1)}, f32[256,1024]{1,0:T(8,128)}, u32[]{:S(2)}) copy-start(f32[256,1024]{1,0:T(8,128)} %all-gather.29.cloned.1.call-done) | copy-start | bytes 3145732
  704.2 53.2 %copy-start.33 = (f32[16]{0:T(128)}, f32[16]{0:T(128)S(1)}, u32[]{:S(2)}) copy-start(f32[16]{0:T(128)S(1)} %div.82) | copy-start | bytes 196
  704.9 89.5 %all-gather.35.cloned.1.call-start = ((), (), s32[]{:S(2)}) async-start(), calls=%async_computation.11 | async-start | bytes 1114112 | tf_op jit(solution)/shard_map/all_gather | solution.py:75
  755.4 74.9 %copy-start.3 = (f32[256,1024]{1,0:T(8,128)S(1)}, f32[256,1024]{1,0:T(8,128)}, u32[]{:S(2)}) copy-start(f32[256,1024]{1,0:T(8,128)} %all-gather.33.cloned.1.call-done) | copy-start | bytes 3145732
Sparse Core Ops, SparseCore 0:
  44.3 44.0 all-gather.12
  113.9 55.2 all-gather.14
  171.1 37.2 all-gather.16
  244.4 39.4 all-gather.18
  314.2 50.4 all-gather.20
  366.4 37.2 all-gather.22
  439.8 39.4 all-gather.24
  509.6 50.3 all-gather.26
  561.8 37.2 all-gather.28
  635.2 39.4 all-gather.30
  705.0 50.3 all-gather.32
  757.1 37.2 all-gather.34
where the time goes:
time: 848 us; the launch traced here: 841 us
  blocking collectives  379 us (45%)
  waiting for transfers between devices  336 us (40%)
  matrix products  64 us (8%)
  local copies, waits for them, and re-layouts  30.5 us (4%)
  other arithmetic  16.4 us (2%)
  between operations  15.3 us (2%)
    all_gather x4, waiting for transfers between devices, local(): resid_piece = lax.all_gather(resid, 'panel', axis=0, tiled=True)  186 us
    all_gather x4, waiting for transfers between devices, local(): dir_piece = lax.all_gather(directions, 'panel', axis=0, tiled=True)  149 us
    psum x4, blocking collectives, local(): sumsq = lax.psum(jnp.sum(rotated * rotated, axis=1), 'dom')  133 us
    psum x4, blocking collectives, local(): lax.psum((jnp.sum(block * block, axis=1), jnp.sum(block * image, axis=1))...  124 us
    all_gather x4, blocking collectives, local(): far = lax.all_gather(outgoing, 'dom', axis=1, tiled=True)  87.8 us
    dot_general x20, matrix products, matmul(): return jnp.dot(left, right, precision=lax.Precision.HIGHEST)  39 us
    psum x1, blocking collectives, local(): sumsq = lax.psum(jnp.sum(start_block * start_block, axis=1), 'dom')  34.2 us
    dot_general x8, matrix products, tile_product(): jnp.einsum('mtk,tjk->mtj', picked, tile_set, precision=lax.Precision.HIGH...  23.2 us
  transfers between devices with their start and end apart: 12, of which 8 were waited for; matrix products, arithmetic and copies ran while one was open for 11% of the time, Pallas kernels for 0%

commit v1 on v0

v1 whole, which is shorter than its diff:
```python
import functools

import jax
import jax.numpy as jnp
from jax import lax
from jax.experimental import pallas as pl
from jax.experimental.pallas import tpu as pltpu
from jax.sharding import PartitionSpec as P

ITERS = 4
MESH = pl.DeviceIdType.MESH
LANES = 128
HALF = 64


def split(value):
    high = value.astype(jnp.bfloat16)
    low = (value - high.astype(jnp.float32)).astype(jnp.bfloat16)
    return high, low


def swap(value):
    return pltpu.roll(value, HALF, value.ndim - 1)


def left_half(shape):
    return lax.broadcasted_iota(jnp.int32, shape, len(shape) - 1) < HALF


def kernel(
    nodes,
    start_hbm,
    prior_hbm,
    degree_hbm,
    tiles_hbm,
    trows_hbm,
    tcols_hbm,
    cuts_hbm,
    count_hbm,
    btiles_hbm,
    brows_hbm,
    bcols_hbm,
    xx_hbm,
    xr_hbm,
    xp_hbm,
    pr_hbm,
    pp_hbm,
    block_ref,
    dirs_ref,
    ritz_ref,
    start_ref,
    prior_ref,
    degree_ref,
    tiles_ref,
    trows,
    tcols,
    cuts_ref,
    count,
    btiles_ref,
    brows,
    bcols,
    rot_ref,
    load_sem,
    onehot,
    weights,
    bweights,
    rotcat,
    yblk,
    yst,
    xblk,
    acc,
    pdir,
    far_out,
    far_in,
    y_out,
    y_in,
    x_out,
    x_in,
    r_out,
    r_in,
    p_out,
    p_in,
    s_out,
    s_in,
    c_out,
    c_in,
    far_send,
    far_recv,
    y_send,
    y_recv,
    x_send,
    x_recv,
    r_send,
    r_recv,
    p_send,
    p_recv,
    s_send,
    s_recv,
    c_send,
    c_recv,
):
    dom, panel = lax.axis_index("dom"), lax.axis_index("panel")
    n_dom, n_panel = lax.axis_size("dom"), lax.axis_size("panel")
    blocks = yblk.shape[0]
    n_tiles, n_bound = weights.shape[0], bweights.shape[0]
    width = yblk.shape[1]

    loads = []

    def load(src, dst):
        copy = pltpu.make_async_copy(src, dst, load_sem.at[len(loads)])
        copy.start()
        loads.append(copy)
        return copy

    got_cuts = load(cuts_hbm, cuts_ref)
    got_count = load(count_hbm, count)
    got_start = load(start_hbm, start_ref)
    got_prior = load(prior_hbm, prior_ref)
    got_index = [
        load(trows_hbm, trows),
        load(tcols_hbm, tcols),
        load(brows_hbm, brows),
        load(bcols_hbm, bcols),
        load(degree_hbm, degree_ref),
    ]
    got_tiles = load(tiles_hbm, tiles_ref)
    got_btiles = load(btiles_hbm, btiles_ref)
    got_rot = [
        load(src, rot_ref.at[at])
        for at, src in enumerate((xx_hbm, xr_hbm, xp_hbm, pr_hbm, pp_hbm))
    ]

    barrier = pltpu.get_barrier_semaphore()
    for step in range(1, n_dom):
        pl.semaphore_signal(
            barrier, inc=1, device_id={"dom": (dom + step) % n_dom}, device_id_type=MESH
        )
    for step in range(1, n_panel):
        pl.semaphore_signal(
            barrier, inc=1, device_id={"panel": (panel + step) % n_panel}, device_id_type=MESH
        )

    def spread(axis, me, n, source, target, send, recv):
        for step in range(1, n):
            peer = (me + step) % n
            pltpu.make_async_remote_copy(
                src_ref=source(peer),
                dst_ref=target(me),
                send_sem=send,
                recv_sem=recv,
                device_id={axis: peer},
                device_id_type=MESH,
            ).start()

    def arrive(like, sem):
        pltpu.make_async_copy(like, like, sem).wait()

    eye = (
        lax.broadcasted_iota(jnp.int32, (width, LANES), 0)
        == lax.broadcasted_iota(jnp.int32, (width, LANES), 1)
    )

    def to_row(partial):
        column = jnp.sum(partial, axis=1, keepdims=True)
        return jnp.sum(jnp.where(eye, column, 0.0), axis=0, keepdims=True)

    def to_column(row):
        return jnp.sum(jnp.where(eye, row, 0.0), axis=1, keepdims=True)

    left8 = left_half((8, LANES))

    def cut_pieces(value):
        top, bottom = value[:8], value[8:]
        return (
            jnp.where(left8, top, swap(bottom)),
            jnp.where(left8, swap(top), bottom),
        )

    def send_panel(pieces_of, out, into, send, recv):
        for b in range(blocks):
            first, second = cut_pieces(pieces_of(b))
            out[2 * b] = first
            out[2 * b + 1] = second
        spread("panel", panel, n_panel, lambda q: out.at[q], lambda q: into.at[q], send, recv)
        into[panel] = out[panel]

    def unpack(into):
        got = into[...]
        turned = swap(got)
        left = left_half(got.shape)
        top = jnp.where(left, got, turned)
        bottom = jnp.where(left, turned, got)
        return jnp.concatenate([top[:, None], bottom[:, None]], axis=1).reshape(-1, LANES)

    def operand(value):
        high = value.astype(jnp.bfloat16).astype(jnp.float32)
        left = left_half(value.shape)
        both = jnp.where(left, high, value - high).astype(jnp.bfloat16)
        only = jnp.where(left, high, 0.0).astype(jnp.bfloat16)
        return jnp.concatenate([both, only], axis=0)

    def rotate(at, stacked):
        return jnp.dot(rotcat[at], stacked, preferred_element_type=jnp.float32)

    def pack(total, out):
        value = total + swap(total)
        value4 = value.reshape(n_panel, 2, 8, LANES)
        out[...] = jnp.where(left_half((n_panel, 8, LANES)), value4[:, 0], value4[:, 1])
        return value

    def assemble(into, put):
        for b in range(blocks):
            first, second = into[2 * b], into[2 * b + 1]
            top = jnp.where(left8, first, swap(second))
            bottom = jnp.where(left8, swap(first), second)
            put(b, jnp.concatenate([top, bottom], axis=0))

    def put_y(b, value):
        yblk[b] = value

    def send_dom(partial, out, into, send, recv):
        out[...] = to_row(partial)
        spread("dom", dom, n_dom, lambda q: out, lambda q: into.at[q], send, recv)
        into[dom] = out[...]

    def total_dom(into, recv):
        arrive(into.at[pl.ds(0, n_dom - 1)], recv)
        return jnp.sum(into[...], axis=0)

    def factor(sumsq):
        return jnp.sqrt(sumsq / nodes + 1e-06)

    got_cuts.wait()
    got_count.wait()
    n_cut = cuts_ref.shape[1]
    cut = jnp.where(
        lax.broadcasted_iota(jnp.int32, (1, n_cut), 1) < count[0], cuts_ref[...], -1
    )
    for b in range(blocks):
        row = lax.broadcasted_iota(jnp.int32, (LANES, n_cut), 0) + b * LANES
        onehot[pl.ds(b * LANES, LANES)] = (row == cut).astype(jnp.float32).astype(jnp.bfloat16)
    got_start.wait()
    for b in range(blocks):
        put_y(b, start_ref[:, b * LANES : (b + 1) * LANES])
    got_prior.wait()

    pl.semaphore_wait(barrier, n_dom + n_panel - 2)

    def tile_step(t, source, weight, row, totals):
        product = lax.dot_general(
            source, weight, (((1,), (1,)), ((), ())), preferred_element_type=jnp.float32
        )
        product = product[:width] + product[width:]
        return tuple(
            total + jnp.where(row == r, product, 0.0) for r, total in enumerate(totals)
        )

    def doubled(value):
        high, low = split(value)
        stacked = jnp.concatenate([high, low], axis=0)
        return jnp.concatenate([stacked, stacked], axis=1)

    def iterate(k, _):
        for b in range(blocks):
            yst[b] = doubled(yblk[b])
        chosen = jnp.zeros((2 * width, n_cut), jnp.float32)
        for b in range(blocks):
            chosen += jnp.dot(
                yst[b, :, :LANES],
                onehot[pl.ds(b * LANES, LANES)],
                preferred_element_type=jnp.float32,
            )
        chosen = chosen[:width] + chosen[width:]
        halves = n_cut // LANES
        for h in range(halves):
            far_out[k, h] = chosen[:, h * LANES : (h + 1) * LANES]
        spread(
            "dom",
            dom,
            n_dom,
            lambda q: far_out.at[k],
            lambda q: far_in.at[k, pl.ds(q * halves, halves)],
            far_send.at[k],
            far_recv.at[k],
        )
        far_in[k, pl.ds(dom * halves, halves)] = far_out[k]

        partial = jnp.zeros((width, LANES), jnp.float32)
        for b in range(blocks):
            partial += yblk[b] * yblk[b]
        send_dom(partial, s_out.at[k], s_in.at[k], s_send.at[k], s_recv.at[k])

        @pl.when(k == 0)
        def _():
            send_panel(
                lambda b: prior_ref[:, b * LANES : (b + 1) * LANES],
                p_out.at[0],
                p_in.at[0],
                p_send.at[0],
                p_recv.at[0],
            )
            for copy in got_index:
                copy.wait()
            got_tiles.wait()

            def prepare(t, _):
                high, low = split(tiles_ref[t])
                weights[t] = jnp.concatenate([high, low], axis=1)
                return 0

            lax.fori_loop(0, n_tiles, prepare, 0)

        def interior(t, totals):
            return tile_step(t, yst[tcols[t]], weights[t], trows[t], totals)

        totals = lax.fori_loop(
            0, n_tiles, interior, (jnp.zeros((width, LANES), jnp.float32),) * blocks
        )
        for b in range(blocks):
            acc[b] = totals[b]

        sumsq = total_dom(s_in.at[k], s_recv.at[k])
        scale = to_column(1.0 / factor(sumsq))
        for b in range(blocks):
            xblk[b] = yblk[b] * scale
        send_panel(lambda b: xblk[b], x_out.at[k], x_in.at[k], x_send.at[k], x_recv.at[k])

        @pl.when(k == 0)
        def _():
            got_btiles.wait()

            def prepare(t, _):
                high, low = split(btiles_ref[t])
                bweights[t] = jnp.concatenate([high, low], axis=1)
                return 0

            lax.fori_loop(0, n_bound, prepare, 0)
            for at, copy in enumerate(got_rot):
                copy.wait()
                high, low = split(rot_ref[at])
                rotcat[at] = jnp.concatenate([high, low], axis=1)
            arrive(p_in.at[0, pl.ds(0, n_panel - 1)], p_recv.at[0])
            pdir[...] = unpack(p_in.at[0])

        arrive(far_in.at[k, pl.ds(0, (n_dom - 1) * halves)], far_recv.at[k])

        def boundary(t, totals):
            source = doubled(far_in[k, bcols[t]])
            return tile_step(t, source, bweights[t], brows[t], totals)

        totals = lax.fori_loop(0, n_bound, boundary, tuple(acc[b] for b in range(blocks)))
        partial = jnp.zeros((width, LANES), jnp.float32)
        for b in range(blocks):
            image = degree_ref[:, b * LANES : (b + 1) * LANES] * yblk[b] - totals[b]
            acc[b] = image
            partial += yblk[b] * image
        send_dom(partial, c_out.at[k], c_in.at[k], c_send.at[k], c_recv.at[k])
        ritz = total_dom(c_in.at[k], c_recv.at[k]) / sumsq
        ritz_ref[...] = ritz
        column = to_column(ritz)
        send_panel(
            lambda b: acc[b] * scale - column * xblk[b],
            r_out.at[k],
            r_in.at[k],
            r_send.at[k],
            r_recv.at[k],
        )

        arrive(x_in.at[k, pl.ds(0, n_panel - 1)], x_recv.at[k])
        old = operand(pdir[...])
        base = rotate(0, operand(unpack(x_in.at[k]))) + rotate(2, old)
        arrive(r_in.at[k, pl.ds(0, n_panel - 1)], r_recv.at[k])
        resid = operand(unpack(r_in.at[k]))
        pack(base + rotate(1, resid), y_out.at[k])
        spread(
            "panel",
            panel,
            n_panel,
            lambda q: y_out.at[k, q],
            lambda q: y_in.at[k, q],
            y_send.at[k],
            y_recv.at[k],
        )
        y_in[k, panel] = y_out[k, panel]

        pdir[...] = pack(rotate(3, resid) + rotate(4, old), p_out.at[1])

        arrive(y_in.at[k, pl.ds(0, n_panel - 1)], y_recv.at[k])
        assemble(y_in.at[k], put_y)
        return 0

    lax.fori_loop(0, ITERS, iterate, 0)

    partial = jnp.zeros((width, LANES), jnp.float32)
    for b in range(blocks):
        partial += yblk[b] * yblk[b]
    send_dom(partial, s_out.at[ITERS], s_in.at[ITERS], s_send.at[ITERS], s_recv.at[ITERS])
    spread(
        "panel",
        panel,
        n_panel,
        lambda q: p_out.at[1, q],
        lambda q: p_in.at[1, q],
        p_send.at[1],
        p_recv.at[1],
    )
    p_in[1, panel] = p_out[1, panel]
    scale = to_column(1.0 / factor(total_dom(s_in.at[ITERS], s_recv.at[ITERS])))
    for b in range(blocks):
        block_ref[:, b * LANES : (b + 1) * LANES] = yblk[b] * scale
    arrive(p_in.at[1, pl.ds(0, n_panel - 1)], p_recv.at[1])

    def put_dirs(b, value):
        dirs_ref[:, b * LANES : (b + 1) * LANES] = value

    assemble(p_in.at[1], put_dirs)

    def left(n, like, sem):
        for _ in range(n - 1):
            arrive(like, sem)

    def drain(k, _):
        left(n_dom, far_out.at[k], far_send.at[k])
        left(n_dom, c_out.at[k], c_send.at[k])
        for out, sem in ((y_out, y_send), (x_out, x_send), (r_out, r_send)):
            arrive(out.at[k, pl.ds(0, n_panel - 1)], sem.at[k])
        return 0

    lax.fori_loop(0, ITERS, drain, 0)

    def drain_self(k, _):
        left(n_dom, s_out.at[k], s_send.at[k])
        return 0

    lax.fori_loop(0, ITERS + 1, drain_self, 0)
    for at in range(2):
        arrive(p_out.at[at, pl.ds(0, n_panel - 1)], p_send.at[at])


def local(n_dom, n_panel, *args):
    start, prior, degree, tiles, trows, tcols, cuts, count, btiles, brows, bcols = args[:11]
    width, ndev = start.shape
    blocks = ndev // LANES
    n_tiles, n_bound, n_cut = tiles.shape[0], btiles.shape[0], cuts.shape[0]
    rows = args[11].shape[0]
    f32, bf16, i32 = jnp.float32, jnp.bfloat16, jnp.int32
    vmem, dma = pltpu.VMEM, pltpu.SemaphoreType.DMA
    n = ITERS

    def smem(shape):
        return pltpu.SMEM(shape, i32)

    def pieces(count):
        return vmem((count, n_panel, 8, LANES), f32)

    scratch = [
        vmem((width, ndev), f32),
        vmem((width, ndev), f32),
        vmem((1, ndev), f32),
        vmem(tiles.shape, f32),
        smem(trows.shape),
        smem(tcols.shape),
        vmem((1, n_cut), i32),
        smem(count.shape),
        vmem(btiles.shape, f32),
        smem(brows.shape),
        smem(bcols.shape),
        vmem((5, rows, rows), f32),
        dma((16,)),
        vmem((ndev, n_cut), bf16),
        vmem((n_tiles, LANES, 2 * LANES), bf16),
        vmem((n_bound, LANES, 2 * LANES), bf16),
        vmem((5, rows, 2 * rows), bf16),
        vmem((blocks, width, LANES), f32),
        vmem((blocks, 2 * width, 2 * LANES), bf16),
        vmem((blocks, width, LANES), f32),
        vmem((blocks, width, LANES), f32),
        vmem((rows, LANES), f32),
        vmem((n, n_cut // LANES, width, LANES), f32),
        vmem((n, n_dom * n_cut // LANES, width, LANES), f32),
        pieces(n),
        pieces(n),
        pieces(n),
        pieces(n),
        pieces(n),
        pieces(n),
        pieces(2),
        pieces(2),
        vmem((n + 1, 1, LANES), f32),
        vmem((n + 1, n_dom, 1, LANES), f32),
        vmem((n, 1, LANES), f32),
        vmem((n, n_dom, 1, LANES), f32),
    ]
    for count_of in (n, n, n, n, 2, n + 1, n):
        scratch += [dma((count_of,)), dma((count_of,))]

    block, dirs, ritz = pl.pallas_call(
        functools.partial(kernel, ndev * n_dom),
        out_shape=(
            jax.ShapeDtypeStruct((width, ndev), f32),
            jax.ShapeDtypeStruct((width, ndev), f32),
            jax.ShapeDtypeStruct((1, LANES), f32),
        ),
        in_specs=[pl.BlockSpec(memory_space=pl.ANY)] * 16,
        out_specs=(pl.BlockSpec(memory_space=pltpu.VMEM),) * 3,
        scratch_shapes=scratch,
        compiler_params=pltpu.CompilerParams(
            collective_id=0, has_side_effects=True, vmem_limit_bytes=48 * 1024 * 1024
        ),
    )(
        start,
        prior,
        degree.reshape(1, -1),
        tiles,
        trows,
        tcols,
        cuts.reshape(1, -1),
        count,
        btiles,
        brows,
        bcols,
        *args[11:],
    )
    return block, dirs, ritz[0, :width]


def solution(mesh):
    return jax.shard_map(
        functools.partial(local, mesh.shape["dom"], mesh.shape["panel"]),
        mesh=mesh,
        in_specs=(
            P("panel", "dom"),
            P("panel", "dom"),
            P("dom"),
            P("dom", None, None),
            P("dom"),
            P("dom"),
            P("dom"),
            P("dom"),
            P("dom", None, None),
            P("dom"),
            P("dom"),
            P(),
            P(),
            P(),
            P(),
            P(),
        ),
        out_specs=(P("panel", "dom"), P("panel", "dom"), P("panel")),
        check_vma=False,
    )
```

time: 848 us -> 135 us (0.16)
  blocking collectives: 379 us -> 0 us
  waiting for transfers between devices: 336 us -> 0 us
  Pallas kernels: 0 us -> 118 us
  matrix products: 64 us -> 0 us
  other arithmetic: 16.4 us -> 0 us
  local copies, waits for them, and re-layouts: 30.5 us -> 15 us
  between operations: 15.3 us -> 1.31 us
    all_gather x12 -> x0, waiting for transfers between devices: 335 us -> none  [the longest x4 186 us: local(): resid_piece = lax.all_gather(resid, 'panel', axis=0, tiled=True)]
    psum x9 -> x0, blocking collectives: 291 us -> none  [the longest x4 133 us: local(): sumsq = lax.psum(jnp.sum(rotated * rotated, axis=1), 'dom')]
    pallas_call x0 -> x1, Pallas kernels: none -> 118 us  [local(): pl.pallas_call(functools.partial(kernel, ndev * n_dom), out_shape=(jax.Sh...]
    all_gather x4 -> x0, blocking collectives: 87.8 us -> none  [local(): far = lax.all_gather(outgoing, 'dom', axis=1, tiled=True)]
    dot_general x36 -> x0, matrix products: 64 us -> none  [the longest x20 39 us: matmul(): return jnp.dot(left, right, precision=lax.Precision.HIGHEST)]
    gather x12 -> x0, local copies, waits for them, and re-layouts: 23.7 us -> none  [the longest x8 15.9 us: tile_product(): picked = jnp.take(blocks, col_ids, axis=1)]
    unnamed x72 -> x32, local copies, waits for them, and re-layouts: 0.21 us -> 14.5 us
  transfers between devices with their start and end apart: 12 -> 0, of which waited for: 8 -> 0; matrix products, arithmetic and copies ran while one was open for 11% -> 0% of each run, Pallas kernels for 0% -> 0%
where the time goes in v1:
time: 135 us; the launch traced here: 134 us
  Pallas kernels  118 us (87%)
  local copies, waits for them, and re-layouts  15 us (11%)
    pallas_call x1, Pallas kernels, local(): pl.pallas_call(functools.partial(kernel, ndev * n_dom), out_shape=(jax.Sh...  118 us
    unnamed x32, local copies, waits for them, and re-layouts  14.5 us

profile of v1, /device:TPU:1, one launch (start us, length us, event | category | flops | bytes accessed | tf_op | source)
XLA Modules:
  0.0 134.4 jit_solution(4078403087462639429)
XLA Ops:
  1.3 0.0 copy-start
  1.3 1.6 %copy-done = f32[32,128,128]{2,1,0:T(8,128)S(1)} copy-done((f32[32,128,128]{2,1,0:T(8,128)S(1)}, f32[32,128,128]{2,1,0:T(8,128)}, u32[]{:S(2)}) %copy-start) | copy-done | bytes 2097176
  2.9 0.0 copy-start.1
  2.9 1.2 copy-done.1
  4.1 0.0 copy-start.2
  4.1 0.9 copy-done.2
  5.1 0.0 copy-start.3
  5.1 0.9 copy-done.3
  6.0 0.0 copy-start.4
  6.0 0.9 copy-done.4
  7.0 0.0 copy-start.5
  7.0 0.9 copy-done.5
  7.9 0.0 copy-start.6
  7.9 0.9 copy-done.6
  8.9 0.0 copy-start.7
  8.9 0.8 copy-done.7
  9.7 0.0 copy-start.8
  9.7 0.8 copy-done.8
  10.5 0.0 copy-start.9
  10.5 0.7 copy-done.9
  11.2 0.0 copy-start.10
  11.2 0.7 copy-done.10
  11.9 0.0 copy-start.11
  11.9 0.7 copy-done.11
  12.6 0.0 copy-start.12
  12.6 0.7 copy-done.12
  13.2 0.0 copy-start.13
  13.2 0.7 copy-done.13
  13.9 0.0 copy-start.14
  13.9 0.7 copy-done.14
  14.5 118.1 %shard_map.175 = (f32[16,1024]{1,0:T(8,128)S(1)}, f32[16,1024]{1,0:T(8,128)S(1)}, f32[1,128]{1,0:T(1,128)S(1)}) custom-call(f32[16,1024]{1,0:T(8,128)S(1)} %copy-done.7, f32[16,1024]{1,0:T(8,128)S(1)} %copy-done.8, f32[1,1024]{1,0:T(1,128)S(1)} %bitcast.4, f32[32,128,128]{2,1,0:T(8,128)S(1)} %copy-done, s32[32]{0:T(128)S(1)} %copy-done.11, ...), custom_call_target="tpu_custom_call" | custom-call | tf_op jit(solution)/shard_map/pallas_call | solution.py:498
  132.6 0.5 slice_bitcast_fusion
  133.1 0.6 copy.22
  133.7 0.6 copy.23
Async XLA Ops:
  1.3 1.6 %copy-start = (f32[32,128,128]{2,1,0:T(8,128)S(1)}, f32[32,128,128]{2,1,0:T(8,128)}, u32[]{:S(2)}) copy-start(f32[32,128,128]{2,1,0:T(8,128)} %tiles_hbm.1) | copy-start | bytes 6291460
  2.9 1.2 copy-start.1
  4.1 0.9 copy-start.2
  5.1 0.9 copy-start.3
  6.0 0.9 copy-start.4
  7.0 0.9 copy-start.5
  7.9 0.9 copy-start.6
  8.9 0.8 copy-start.7
  9.7 0.8 copy-start.8
  10.5 0.7 copy-start.9
  11.2 0.7 copy-start.10
  11.9 0.7 copy-start.11
  12.6 0.7 copy-start.12
  13.2 0.7 copy-start.13
  13.9 0.7 copy-start.14

commit v2 on v0

v2 whole, which is shorter than its diff:
```python
import functools

import jax
import jax.numpy as jnp
from jax import lax
from jax.experimental import pallas as pl
from jax.experimental.pallas import tpu as pltpu
from jax.sharding import PartitionSpec as P

ITERS = 4
MESH = pl.DeviceIdType.MESH
LANES = 128
HALF = 64
UNROLL = 8
K, Q = 0, 1
SHIFT = 2.5


def split(value):
    high = value.astype(jnp.bfloat16)
    low = (value - high.astype(jnp.float32)).astype(jnp.bfloat16)
    return high, low


def swap(value):
    return pltpu.roll(value, HALF, value.ndim - 1)


def left_half(shape):
    return lax.broadcasted_iota(jnp.int32, shape, len(shape) - 1) < HALF


def dot(left, right):
    return jnp.dot(left, right, preferred_element_type=jnp.float32)


def dot_transposed(left, right):
    return lax.dot_general(
        left, right, (((1,), (1,)), ((), ())), preferred_element_type=jnp.float32
    )


def kernel(
    nodes,
    start_hbm,
    prior_hbm,
    degree_hbm,
    tiles_hbm,
    trows_hbm,
    tcols_hbm,
    cuts_hbm,
    count_hbm,
    btiles_hbm,
    brows_hbm,
    bcols_hbm,
    xx_hbm,
    xr_hbm,
    xp_hbm,
    pr_hbm,
    pp_hbm,
    block_ref,
    dirs_ref,
    ritz_ref,
    start_ref,
    prior_ref,
    degree_ref,
    tiles_ref,
    trows,
    tcols,
    cuts_ref,
    count,
    btiles_ref,
    brows,
    bcols,
    rot_ref,
    load_sem,
    onehot,
    weights,
    bweights,
    xp_cat,
    pp_cat,
    y_cat,
    p_cat,
    field,
    stacked,
    acc,
    y_data,
    p_data,
    far_out,
    far_in,
    move_out,
    move_in,
    sum_out,
    sum_in,
    far_send,
    far_recv,
    move_send,
    move_recv,
    sum_send,
    sum_recv,
):
    dom, panel = lax.axis_index("dom"), lax.axis_index("panel")
    n_dom, n_panel = lax.axis_size("dom"), lax.axis_size("panel")
    blocks, width = field.shape[1], field.shape[2]
    n_tiles, n_bound = weights.shape[0], bweights.shape[0]
    rows = rot_ref.shape[1]
    n_cut = cuts_ref.shape[1]
    halves = n_cut // LANES
    f32, bf16 = jnp.float32, jnp.bfloat16

    loads = []

    def load(src, dst):
        copy = pltpu.make_async_copy(src, dst, load_sem.at[len(loads)])
        copy.start()
        loads.append(copy)
        return copy

    got_cuts = load(cuts_hbm, cuts_ref)
    got_count = load(count_hbm, count)
    got_start = load(start_hbm, start_ref)
    got_prior = load(prior_hbm, prior_ref)
    got_index = [
        load(trows_hbm, trows),
        load(tcols_hbm, tcols),
        load(brows_hbm, brows),
        load(bcols_hbm, bcols),
        load(degree_hbm, degree_ref),
    ]
    got_tiles = load(tiles_hbm, tiles_ref)
    got_btiles = load(btiles_hbm, btiles_ref)
    got_rot = [
        load(src, rot_ref.at[at])
        for at, src in enumerate((xx_hbm, xr_hbm, xp_hbm, pr_hbm, pp_hbm))
    ]

    barrier = pltpu.get_barrier_semaphore()
    for step in range(1, n_dom):
        pl.semaphore_signal(
            barrier, inc=1, device_id={"dom": (dom + step) % n_dom}, device_id_type=MESH
        )
    for step in range(1, n_panel):
        pl.semaphore_signal(
            barrier, inc=1, device_id={"panel": (panel + step) % n_panel}, device_id_type=MESH
        )

    def spread(axis, source, target, send, recv):
        me, n = (dom, n_dom) if axis == "dom" else (panel, n_panel)
        for step in range(1, n):
            peer = (me + step) % n
            pltpu.make_async_remote_copy(
                src_ref=source(peer),
                dst_ref=target(me),
                send_sem=send,
                recv_sem=recv,
                device_id={axis: peer},
                device_id_type=MESH,
            ).start()

    def arrive(like, sem):
        pltpu.make_async_copy(like, like, sem).wait()


    def set_block(kind, b, value):
        field[kind, b] = value
        high, low = split(value)
        both = jnp.concatenate([high, low], axis=0)
        at = kind * 2 * width
        stacked[b, at : at + 2 * width] = jnp.concatenate([both, both], axis=1)

    def send_far(kind, j):
        at = kind * 2 * width
        chosen = jnp.zeros((2 * width, n_cut), f32)
        for b in range(blocks):
            chosen += dot(
                stacked[b, at : at + 2 * width, :LANES], onehot[b * LANES : (b + 1) * LANES]
            )
        chosen = chosen[:width] + chosen[width:]
        slot = 2 * j + kind
        for h in range(halves):
            far_out[slot, h] = chosen[:, h * LANES : (h + 1) * LANES]
        spread(
            "dom",
            lambda q: far_out.at[slot],
            lambda q: far_in[slot].at[pl.ds(q * halves, halves)],
            far_send.at[slot],
            far_recv.at[slot],
        )
        far_in[slot][pl.ds(dom * halves, halves)] = far_out[slot]

    def collect(totals, products, row_ids):
        totals = list(totals)
        for product, row in zip(products, row_ids):
            for r in range(blocks):
                totals[r] = totals[r] + jnp.where(row == r, product, 0.0)
        return tuple(totals)

    def interior(kinds):
        wide = 2 * width * len(kinds)

        def step(i, totals):
            products, row_ids = [], []
            for u in range(min(UNROLL, n_tiles)):
                t = i * min(UNROLL, n_tiles) + u
                product = dot_transposed(stacked[tcols[t], :wide], weights[t])
                parts = [
                    product[2 * width * n : 2 * width * n + width]
                    + product[2 * width * n + width : 2 * width * (n + 1)]
                    for n in range(len(kinds))
                ]
                products.append(jnp.concatenate(parts, axis=0))
                row_ids.append(trows[t])
            return collect(totals, products, row_ids)

        zero = jnp.zeros((width * len(kinds), LANES), f32)
        totals = lax.fori_loop(0, n_tiles // min(UNROLL, n_tiles), step, (zero,) * blocks)
        for b in range(blocks):
            for n in range(len(kinds)):
                acc[n, b] = totals[b][n * width : (n + 1) * width]

    def boundary(kind, j):
        slot = 2 * j + kind
        arrive(far_in[slot].at[pl.ds(0, (n_dom - 1) * halves)], far_recv.at[slot])

        def step(i, totals):
            products, row_ids = [], []
            for u in range(min(UNROLL, n_bound)):
                t = i * min(UNROLL, n_bound) + u
                high, low = split(far_in[slot][bcols[t]])
                both = jnp.concatenate([high, low], axis=0)
                product = dot_transposed(jnp.concatenate([both, both], axis=1), bweights[t])
                products.append(product[:width] + product[width:])
                row_ids.append(brows[t])
            return collect(totals, products, row_ids)

        totals = lax.fori_loop(
            0,
            n_bound // min(UNROLL, n_bound),
            step,
            tuple(acc[kind, b] for b in range(blocks)),
        )
        return [
            (degree_ref[:, b * LANES : (b + 1) * LANES] - SHIFT) * field[kind, b] - totals[b]
            for b in range(blocks)
        ]

    left8 = left_half((8, LANES))

    def send_nodes(slot, values):
        for b in range(blocks):
            value = values(b)
            top, bottom = value[:8], value[8:]
            move_out[slot, 2 * b] = jnp.where(left8, top, swap(bottom))
            move_out[slot, 2 * b + 1] = jnp.where(left8, swap(top), bottom)
        move(slot)

    def move(slot):
        spread(
            "panel",
            lambda q: move_out.at[slot, q],
            lambda q: move_in.at[slot, q],
            move_send.at[slot],
            move_recv.at[slot],
        )
        move_in[slot, panel] = move_out[slot, panel]

    def wait_move(slot):
        arrive(move_in.at[slot, pl.ds(0, n_panel - 1)], move_recv.at[slot])

    def assemble(slot, put):
        for b in range(blocks):
            first, second = move_in[slot, 2 * b], move_in[slot, 2 * b + 1]
            top = jnp.where(left8, first, swap(second))
            bottom = jnp.where(left8, swap(first), second)
            put(b, jnp.concatenate([top, bottom], axis=0))


    def unpack(slot):
        got = move_in[slot]
        turned = swap(got)
        left = left_half(got.shape)
        top = jnp.where(left, got, turned)
        bottom = jnp.where(left, turned, got)
        return jnp.concatenate([top[:, None], bottom[:, None]], axis=1).reshape(rows, LANES)

    left_rows = left_half((rows, LANES))

    def put_operand(data, at, j, value):
        high = value.astype(bf16).astype(f32)
        lanes = slice(j * LANES, (j + 1) * LANES)
        data[at, :rows, lanes] = jnp.where(left_rows, high, value - high).astype(bf16)
        data[at, rows:, lanes] = jnp.where(left_rows, high, 0.0).astype(bf16)

    def receive(data, slot, j):
        wait_move(slot)
        put_operand(data, 0, j, unpack(slot))

    def put_matrix(ref, at, matrix):
        high, low = split(matrix)
        ref[:, at * 2 * rows : at * 2 * rows + rows] = high
        ref[:, at * 2 * rows + rows : (at + 1) * 2 * rows] = low

    def rotate(matrices, from_cat, k, first, count):
        now = k % 2
        lo, hi = first * LANES, (first + count) * LANES
        total = dot(matrices[:, : 2 * rows], y_data[now, :, lo:hi])
        total += dot(matrices[:, 2 * rows :], y_data[now, :, lo + LANES : hi + LANES])
        total += dot(from_cat[...], p_data[now, :, lo:hi])
        values = []
        for n in range(count):
            part = total[:, n * LANES : (n + 1) * LANES]
            values.append(part + swap(part))
        return values

    def pack(slot, value):
        value4 = value.reshape(n_panel, 2, 8, LANES)
        move_out[slot] = jnp.where(
            left_half((n_panel, 8, LANES)), value4[:, 0], value4[:, 1]
        )


    def send_sum(axis, slot, value):
        sum_out[slot] = value
        spread(
            axis,
            lambda q: sum_out.at[slot],
            lambda q: sum_in.at[slot, q],
            sum_send.at[slot],
            sum_recv.at[slot],
        )
        sum_in[slot, dom if axis == "dom" else panel] = value

    def wait_sum(axis, slot):
        n = n_dom if axis == "dom" else n_panel
        arrive(sum_in.at[slot, pl.ds(0, n - 1)], sum_recv.at[slot])
        return jnp.sum(sum_in[slot, :n], axis=0)

    own = lax.broadcasted_iota(jnp.int32, (width, rows), 1) == (
        lax.broadcasted_iota(jnp.int32, (width, rows), 0) + panel * width
    )

    def to_row(partial):
        column = jnp.sum(partial, axis=1, keepdims=True)
        return jnp.sum(jnp.where(own, column, 0.0), axis=0, keepdims=True)

    def to_column(row):
        return jnp.sum(jnp.where(own, row, 0.0), axis=1, keepdims=True)

    pick_row = lax.broadcasted_iota(jnp.int32, (width, 2 * LANES), 0)
    pick_lane = lax.broadcasted_iota(jnp.int32, (width, 2 * LANES), 1) // HALF % 2
    pick = (pick_row == pick_lane).astype(f32).astype(bf16)

    def node_sums(first, second):
        product = first * jnp.where(left_rows, first, second)
        high, low = split(product)
        return dot_transposed(pick, jnp.concatenate([high, low], axis=1))[:2]

    def inverse_factor(total):
        return 1.0 / jnp.sqrt(total[0:1] / nodes + 1e-06)


    got_cuts.wait()
    got_count.wait()
    cut = jnp.where(
        lax.broadcasted_iota(jnp.int32, (1, n_cut), 1) < count[0], cuts_ref[...], -1
    )
    for b in range(blocks):
        row = lax.broadcasted_iota(jnp.int32, (LANES, n_cut), 0) + b * LANES
        onehot[b * LANES : (b + 1) * LANES] = (row == cut).astype(f32).astype(bf16)
    got_start.wait()
    for b in range(blocks):
        set_block(K, b, start_ref[:, b * LANES : (b + 1) * LANES])
    got_prior.wait()
    for b in range(blocks):
        set_block(Q, b, prior_ref[:, b * LANES : (b + 1) * LANES])

    pl.semaphore_wait(barrier, n_dom + n_panel - 2)

    send_far(K, 0)
    send_far(Q, 0)
    send_nodes(0, lambda b: field[K, b])
    send_nodes(1, lambda b: field[Q, b])

    def split_tiles(source, target):
        def step(t, _):
            high, low = split(source[t])
            target[t] = jnp.concatenate([high, low], axis=1)
            return 0

        lax.fori_loop(0, source.shape[0], step, 0)

    for copy in got_index:
        copy.wait()
    got_tiles.wait()
    split_tiles(tiles_ref, weights)
    got_btiles.wait()
    split_tiles(btiles_ref, bweights)
    interior((K, Q))

    def advance(kind, j):
        images = boundary(kind, j)
        if kind == K and j == 0:
            square = jnp.zeros((width, LANES), f32)
            cross = jnp.zeros((width, LANES), f32)
            for b in range(blocks):
                square += field[K, b] * field[K, b]
                cross += field[K, b] * images[b]
            send_sum("dom", 0, jnp.concatenate([to_row(square), to_row(cross)], axis=0))
        for b in range(blocks):
            set_block(kind, b, images[b])
        if j + 1 < ITERS - kind:
            send_far(kind, j + 1)
        send_nodes(2 * (j + 1) + kind, lambda b: field[kind, b])

    advance(K, 0)
    advance(Q, 0)
    interior((K, Q))
    for copy in got_rot:
        copy.wait()
    put_matrix(xp_cat, 0, rot_ref[2])
    put_matrix(pp_cat, 0, rot_ref[4])
    receive(y_data, 0, 0)
    receive(p_data, 1, 0)
    send_sum("panel", 1, wait_sum("dom", 0))
    receive(y_data, 2, 1)
    receive(p_data, 3, 1)
    advance(K, 1)
    advance(Q, 1)

    f_block, f_dirs = 2 * ITERS + 1, 2 * ITERS + 2
    for k in range(ITERS):
        depth = ITERS - k
        slot = 2 * k + 1
        total = wait_sum("panel" if k == 0 else "dom", slot)
        scale = inverse_factor(total)
        ritz = total[1:2] / total[0:1]
        xr_scaled = rot_ref[1] * scale
        put_matrix(y_cat, 0, rot_ref[0] * scale - xr_scaled * ritz)
        put_matrix(y_cat, 1, xr_scaled)
        if k == 0:
            receive(y_data, 4, 2)
        now = rotate(y_cat, xp_cat, k, 0, min(2, depth))
        nxt = (k + 1) % 2
        if depth > 1:
            send_sum("panel", slot + 1, node_sums(now[0], now[1]))
            for n in range(2):
                put_operand(y_data, nxt, n, now[n])
        else:
            send_sum("panel", slot + 1, node_sums(now[0], now[0]))
            pack(f_block, now[0])
            move(f_block)
        pr_scaled = rot_ref[3] * scale
        put_matrix(p_cat, 0, -pr_scaled * ritz)
        put_matrix(p_cat, 1, pr_scaled)
        if depth > 1:
            first = rotate(p_cat, pp_cat, k, 0, min(2, depth - 1))
            for n, value in enumerate(first):
                put_operand(p_data, nxt, n, value)
        else:
            pack(f_dirs, rotate(p_cat, pp_cat, k, 0, 1)[0])
            move(f_dirs)
        if k == 0:
            interior((K, Q))
            advance(K, 2)
            advance(Q, 2)
            receive(p_data, 5, 2)
            receive(y_data, 6, 3)
            receive(p_data, 7, 3)
        if depth > 2:
            if k == 0:
                send_sum("dom", slot + 2, wait_sum("panel", slot + 1))
                interior((K,))
                advance(K, 3)
                receive(y_data, 8, 4)
            for n in range(2, depth):
                put_operand(y_data, nxt, n, rotate(y_cat, xp_cat, k, n, 1)[0])
            for n in range(2, depth - 1):
                put_operand(p_data, nxt, n, rotate(p_cat, pp_cat, k, n, 1)[0])
        if k > 0:
            send_sum("dom", slot + 2, wait_sum("panel", slot + 1))

    ritz_column = to_column(ritz + SHIFT)
    narrow = lax.broadcasted_iota(jnp.int32, (width, LANES), 1) == lax.broadcasted_iota(
        jnp.int32, (width, LANES), 0
    )
    ritz_ref[...] = jnp.sum(jnp.where(narrow, ritz_column, 0.0), axis=0, keepdims=True)

    def put_dirs(b, value):
        dirs_ref[:, b * LANES : (b + 1) * LANES] = value

    wait_move(f_dirs)
    assemble(f_dirs, put_dirs)
    wait_move(f_block)
    scale = to_column(inverse_factor(wait_sum("dom", 2 * ITERS + 1)))

    def put_block(b, value):
        block_ref[:, b * LANES : (b + 1) * LANES] = value * scale

    assemble(f_block, put_block)

    def drain(out, sem, n, whole):
        def step(slot, _):
            if whole:
                for _ in range(n - 1):
                    arrive(out.at[slot], sem.at[slot])
            else:
                arrive(out.at[slot, pl.ds(0, n - 1)], sem.at[slot])
            return 0

        lax.fori_loop(0, out.shape[0], step, 0)

    drain(far_out, far_send, n_dom, True)
    drain(move_out, move_send, n_panel, False)
    for slot in range(2 * ITERS + 2):
        n = n_panel if slot in (1, 2, 4, 6, 8) else n_dom
        for _ in range(n - 1):
            arrive(sum_out.at[slot], sum_send.at[slot])


def local(n_dom, n_panel, *args):
    start, prior, degree, tiles, trows, tcols, cuts, count, btiles, brows, bcols = args[:11]
    width, ndev = start.shape
    blocks = ndev // LANES
    n_tiles, n_bound, n_cut = tiles.shape[0], btiles.shape[0], cuts.shape[0]
    rows = args[11].shape[0]
    f32, bf16, i32 = jnp.float32, jnp.bfloat16, jnp.int32
    vmem, dma = pltpu.VMEM, pltpu.SemaphoreType.DMA
    n_far, n_move, n_sum = 2 * ITERS - 1, 2 * ITERS + 3, 2 * ITERS + 2

    def smem(shape):
        return pltpu.SMEM(shape, i32)

    scratch = [
        vmem((width, ndev), f32),
        vmem((width, ndev), f32),
        vmem((1, ndev), f32),
        vmem(tiles.shape, f32),
        smem(trows.shape),
        smem(tcols.shape),
        vmem((1, n_cut), i32),
        smem(count.shape),
        vmem(btiles.shape, f32),
        smem(brows.shape),
        smem(bcols.shape),
        vmem((5, rows, rows), f32),
        dma((16,)),
        vmem((ndev, n_cut), bf16),
        vmem((n_tiles, LANES, 2 * LANES), bf16),
        vmem((n_bound, LANES, 2 * LANES), bf16),
        vmem((rows, 2 * rows), bf16),
        vmem((rows, 2 * rows), bf16),
        vmem((rows, 4 * rows), bf16),
        vmem((rows, 4 * rows), bf16),
        vmem((2, blocks, width, LANES), f32),
        vmem((blocks, 4 * width, 2 * LANES), bf16),
        vmem((2, blocks, width, LANES), f32),
        vmem((2, 2 * rows, (ITERS + 1) * LANES), bf16),
        vmem((2, 2 * rows, ITERS * LANES), bf16),
        vmem((n_far, n_cut // LANES, width, LANES), f32),
        (vmem((n_dom * n_cut // LANES, width, LANES), f32),) * n_far,
        vmem((n_move, n_panel, 8, LANES), f32),
        vmem((n_move, n_panel, 8, LANES), f32),
        vmem((n_sum, 2, rows), f32),
        vmem((n_sum, max(n_dom, n_panel), 2, rows), f32),
    ]
    for slots in (n_far, n_move, n_sum):
        scratch += [dma((slots,)), dma((slots,))]

    block, dirs, ritz = pl.pallas_call(
        functools.partial(kernel, ndev * n_dom),
        out_shape=(
            jax.ShapeDtypeStruct((width, ndev), f32),
            jax.ShapeDtypeStruct((width, ndev), f32),
            jax.ShapeDtypeStruct((1, LANES), f32),
        ),
        in_specs=[pl.BlockSpec(memory_space=pl.ANY)] * 16,
        out_specs=(pl.BlockSpec(memory_space=pltpu.VMEM),) * 3,
        scratch_shapes=scratch,
        compiler_params=pltpu.CompilerParams(
            collective_id=0, has_side_effects=True, vmem_limit_bytes=60 * 1024 * 1024
        ),
    )(
        start,
        prior,
        degree.reshape(1, -1),
        tiles,
        trows,
        tcols,
        cuts.reshape(1, -1),
        count,
        btiles,
        brows,
        bcols,
        *args[11:],
    )
    return block, dirs, ritz[0, :width]


def solution(mesh):
    return jax.shard_map(
        functools.partial(local, mesh.shape["dom"], mesh.shape["panel"]),
        mesh=mesh,
        in_specs=(
            P("panel", "dom"),
            P("panel", "dom"),
            P("dom"),
            P("dom", None, None),
            P("dom"),
            P("dom"),
            P("dom"),
            P("dom"),
            P("dom", None, None),
            P("dom"),
            P("dom"),
            P(),
            P(),
            P(),
            P(),
            P(),
        ),
        out_specs=(P("panel", "dom"), P("panel", "dom"), P("panel")),
        check_vma=False,
    )
```

time: 848 us -> 89.1 us (0.11)
  blocking collectives: 379 us -> 0 us
  waiting for transfers between devices: 336 us -> 0 us
  Pallas kernels: 0 us -> 83.5 us
  matrix products: 64 us -> 0 us
  local copies, waits for them, and re-layouts: 30.5 us -> 4.12 us
  other arithmetic: 16.4 us -> 0 us
  between operations: 15.3 us -> 1.29 us
    all_gather x12 -> x0, waiting for transfers between devices: 335 us -> none  [the longest x4 186 us: local(): resid_piece = lax.all_gather(resid, 'panel', axis=0, tiled=True)]
    psum x9 -> x0, blocking collectives: 291 us -> none  [the longest x4 133 us: local(): sumsq = lax.psum(jnp.sum(rotated * rotated, axis=1), 'dom')]
    all_gather x4 -> x0, blocking collectives: 87.8 us -> none  [local(): far = lax.all_gather(outgoing, 'dom', axis=1, tiled=True)]
    pallas_call x0 -> x1, Pallas kernels: none -> 83.5 us  [local(): pl.pallas_call(functools.partial(kernel, ndev * n_dom), out_shape=(jax.Sh...]
    dot_general x36 -> x0, matrix products: 64 us -> none  [the longest x20 39 us: matmul(): return jnp.dot(left, right, precision=lax.Precision.HIGHEST)]
    gather x12 -> x0, local copies, waits for them, and re-layouts: 23.7 us -> none  [the longest x8 15.9 us: tile_product(): picked = jnp.take(blocks, col_ids, axis=1)]
  transfers between devices with their start and end apart: 12 -> 0, of which waited for: 8 -> 0; matrix products, arithmetic and copies ran while one was open for 11% -> 0% of each run, Pallas kernels for 0% -> 0%
where the time goes in v2:
time: 89.1 us; the launch traced here: 88.9 us
  Pallas kernels  83.5 us (94%)
  local copies, waits for them, and re-layouts  4.12 us (5%)
  between operations  1.29 us (1%)
    pallas_call x1, Pallas kernels, local(): pl.pallas_call(functools.partial(kernel, ndev * n_dom), out_shape=(jax.Sh...  83.5 us
    unnamed x2, local copies, waits for them, and re-layouts  2.95 us

profile of v2, /device:TPU:1, one launch (start us, length us, event | category | flops | bytes accessed | tf_op | source)
XLA Modules:
  0.0 88.9 jit_solution(9989953354829672844)
XLA Ops:
  1.3 83.5 %shard_map.175 = (f32[16,1024]{1,0:T(8,128)}, f32[16,1024]{1,0:T(8,128)}, f32[1,128]{1,0:T(1,128)}) custom-call(f32[16,1024]{1,0:T(8,128)} %start_hbm.1, f32[16,1024]{1,0:T(8,128)} %prior_hbm.1, f32[1,1024]{1,0:T(1,128)} %bitcast.4, f32[32,128,128]{2,1,0:T(8,128)} %tiles_hbm.1, s32[32]{0:T(128)} %trows_hbm.1, s32[32]{0:T(128)} %tcols_hbm.1, ...), custom_call_target="tpu_custom_call" | custom-call | tf_op jit(solution)/shard_map/pallas_call | solution.py:569
  84.7 1.2 %slice_bitcast_fusion = f32[16]{0:T(128)} fusion(f32[1,128]{1,0:T(1,128)} %get-tuple-element.8), kind=kLoop, calls=%fused_computation | loop fusion | bytes 128 | tf_op jit(solution)/shard_map/squeeze | solution.py:596
  85.9 1.5 %copy.22 = f32[16,1024]{1,0:T(8,128)} copy(f32[16,1024]{1,0:T(8,128)} %get-tuple-element.12) | data formatting | bytes 131072
  87.4 1.5 %copy.23 = f32[16,1024]{1,0:T(8,128)} copy(f32[16,1024]{1,0:T(8,128)} %get-tuple-element.13) | data formatting | bytes 131072

commit v3 on v2

--- a/solution.py
+++ b/solution.py
@@ -1,4 +1,5 @@
 import functools
+import math
 
 import jax
 import jax.numpy as jnp
@@ -11,7 +12,7 @@
 MESH = pl.DeviceIdType.MESH
 LANES = 128
 HALF = 64
-UNROLL = 8
+UNROLL = 16
 K, Q = 0, 1
 SHIFT = 2.5
 
@@ -108,6 +109,25 @@
     halves = n_cut // LANES
     f32, bf16 = jnp.float32, jnp.bfloat16
 
+    side = math.isqrt(n_dom)
+    dom_y, dom_x = dom // side, dom % side
+    panel_z, core = panel // 2, panel % 2
+    dom_steps = [(y, x) for y in range(n_dom // side) for x in range(side)][1:]
+    dom_steps.sort(key=lambda s: -min(s[0], n_dom // side - s[0]) - min(s[1], side - s[1]))
+    panel_steps = [(z, c) for z in range(n_panel // 2) for c in range(2)][1:]
+    panel_steps.sort(key=lambda s: -min(s[0], n_panel // 2 - s[0]))
+    peers = {
+        "dom": [
+            (dom_y + y) % (n_dom // side) * side + (dom_x + x) % side for y, x in dom_steps
+        ],
+        "panel": [(panel_z + z) % (n_panel // 2) * 2 + (core + c) % 2 for z, c in panel_steps],
+    }
+
+    barrier = pltpu.get_barrier_semaphore()
+    for axis in ("dom", "panel"):
+        for peer in peers[axis]:
+            pl.semaphore_signal(barrier, inc=1, device_id={axis: peer}, device_id_type=MESH)
+
     loads = []
 
     def load(src, dst):
@@ -134,20 +154,9 @@
         for at, src in enumerate((xx_hbm, xr_hbm, xp_hbm, pr_hbm, pp_hbm))
     ]
 
-    barrier = pltpu.get_barrier_semaphore()
-    for step in range(1, n_dom):
-        pl.semaphore_signal(
-            barrier, inc=1, device_id={"dom": (dom + step) % n_dom}, device_id_type=MESH
-        )
-    for step in range(1, n_panel):
-        pl.semaphore_signal(
-            barrier, inc=1, device_id={"panel": (panel + step) % n_panel}, device_id_type=MESH
-        )
-
     def spread(axis, source, target, send, recv):
-        me, n = (dom, n_dom) if axis == "dom" else (panel, n_panel)
-        for step in range(1, n):
-            peer = (me + step) % n
+        me = dom if axis == "dom" else panel
+        for peer in peers[axis]:
             pltpu.make_async_remote_copy(
                 src_ref=source(peer),
                 dst_ref=target(me),
@@ -168,7 +177,7 @@
         at = kind * 2 * width
         stacked[b, at : at + 2 * width] = jnp.concatenate([both, both], axis=1)
 
-    def send_far(kind, j):
+    def choose(kind, j):
         at = kind * 2 * width
         chosen = jnp.zeros((2 * width, n_cut), f32)
         for b in range(blocks):
@@ -179,6 +188,9 @@
         slot = 2 * j + kind
         for h in range(halves):
             far_out[slot, h] = chosen[:, h * LANES : (h + 1) * LANES]
+
+    def send_far(kind, j):
+        slot = 2 * j + kind
         spread(
             "dom",
             lambda q: far_out.at[slot],
@@ -299,6 +311,33 @@
         high, low = split(matrix)
         ref[:, at * 2 * rows : at * 2 * rows + rows] = high
         ref[:, at * 2 * rows + rows : (at + 1) * 2 * rows] = low
+
+    def scale_matrices(k, total):
+        scale = inverse_factor(total)
+        ritz = total[1:2] / total[0:1]
+        xr_scaled = rot_ref[1] * scale
+        put_matrix(y_cat.at[k % 2], 0, rot_ref[0] * scale - xr_scaled * ritz)
+        put_matrix(y_cat.at[k % 2], 1, xr_scaled)
+        return scale, ritz
+
+    def scale_direction_matrices(scale, ritz):
+        pr_scaled = rot_ref[3] * scale
+        put_matrix(p_cat, 0, -pr_scaled * ritz)
+        put_matrix(p_cat, 1, pr_scaled)
+
+    def new_y(k, first, count):
+        return rotate(y_cat.at[k % 2], xp_cat, k, first, count)
+
+    def new_p(k, first, count):
+        return rotate(p_cat, pp_cat, k, first, count)
+
+    def put_y(k, first, values):
+        for n, value in enumerate(values):
+            put_operand(y_data, (k + 1) % 2, first + n, value)
+
+    def put_p(k, first, values):
+        for n, value in enumerate(values):
+            put_operand(p_data, (k + 1) % 2, first + n, value)
 
     def rotate(matrices, from_cat, k, first, count):
         now = k % 2
@@ -374,12 +413,9 @@
     for b in range(blocks):
         set_block(Q, b, prior_ref[:, b * LANES : (b + 1) * LANES])
 
+    choose(K, 0)
+    choose(Q, 0)
     pl.semaphore_wait(barrier, n_dom + n_panel - 2)
-
-    send_far(K, 0)
-    send_far(Q, 0)
-    send_nodes(0, lambda b: field[K, b])
-    send_nodes(1, lambda b: field[Q, b])
 
     def split_tiles(source, target):
         def step(t, _):
@@ -389,95 +425,106 @@
 
         lax.fori_loop(0, source.shape[0], step, 0)
 
-    for copy in got_index:
-        copy.wait()
-    got_tiles.wait()
-    split_tiles(tiles_ref, weights)
-    got_btiles.wait()
-    split_tiles(btiles_ref, bweights)
-    interior((K, Q))
-
     def advance(kind, j):
         images = boundary(kind, j)
+        square = jnp.zeros((width, LANES), f32)
+        cross = jnp.zeros((width, LANES), f32)
         if kind == K and j == 0:
-            square = jnp.zeros((width, LANES), f32)
-            cross = jnp.zeros((width, LANES), f32)
             for b in range(blocks):
                 square += field[K, b] * field[K, b]
                 cross += field[K, b] * images[b]
-            send_sum("dom", 0, jnp.concatenate([to_row(square), to_row(cross)], axis=0))
         for b in range(blocks):
             set_block(kind, b, images[b])
         if j + 1 < ITERS - kind:
+            choose(kind, j + 1)
             send_far(kind, j + 1)
+        if kind == K and j == 0:
+            send_sum("dom", 0, jnp.concatenate([to_row(square), to_row(cross)], axis=0))
         send_nodes(2 * (j + 1) + kind, lambda b: field[kind, b])
 
+    f_block, f_dirs = 2 * ITERS + 1, 2 * ITERS + 2
+
+    send_far(K, 0)
+    send_nodes(0, lambda b: field[K, b])
+    got_tiles.wait()
+    split_tiles(tiles_ref, weights)
+    send_far(Q, 0)
+    send_nodes(1, lambda b: field[Q, b])
+    got_btiles.wait()
+    split_tiles(btiles_ref, bweights)
+    for copy in got_index:
+        copy.wait()
+    interior((K, Q))
     advance(K, 0)
-    advance(Q, 0)
-    interior((K, Q))
     for copy in got_rot:
         copy.wait()
     put_matrix(xp_cat, 0, rot_ref[2])
     put_matrix(pp_cat, 0, rot_ref[4])
     receive(y_data, 0, 0)
     receive(p_data, 1, 0)
+    advance(Q, 0)
+    interior((K, Q))
     send_sum("panel", 1, wait_sum("dom", 0))
     receive(y_data, 2, 1)
     receive(p_data, 3, 1)
     advance(K, 1)
     advance(Q, 1)
 
-    f_block, f_dirs = 2 * ITERS + 1, 2 * ITERS + 2
-    for k in range(ITERS):
-        depth = ITERS - k
-        slot = 2 * k + 1
-        total = wait_sum("panel" if k == 0 else "dom", slot)
-        scale = inverse_factor(total)
-        ritz = total[1:2] / total[0:1]
-        xr_scaled = rot_ref[1] * scale
-        put_matrix(y_cat, 0, rot_ref[0] * scale - xr_scaled * ritz)
-        put_matrix(y_cat, 1, xr_scaled)
-        if k == 0:
-            receive(y_data, 4, 2)
-        now = rotate(y_cat, xp_cat, k, 0, min(2, depth))
-        nxt = (k + 1) % 2
-        if depth > 1:
-            send_sum("panel", slot + 1, node_sums(now[0], now[1]))
-            for n in range(2):
-                put_operand(y_data, nxt, n, now[n])
-        else:
-            send_sum("panel", slot + 1, node_sums(now[0], now[0]))
-            pack(f_block, now[0])
-            move(f_block)
-        pr_scaled = rot_ref[3] * scale
-        put_matrix(p_cat, 0, -pr_scaled * ritz)
-        put_matrix(p_cat, 1, pr_scaled)
-        if depth > 1:
-            first = rotate(p_cat, pp_cat, k, 0, min(2, depth - 1))
-            for n, value in enumerate(first):
-                put_operand(p_data, nxt, n, value)
-        else:
-            pack(f_dirs, rotate(p_cat, pp_cat, k, 0, 1)[0])
-            move(f_dirs)
-        if k == 0:
-            interior((K, Q))
-            advance(K, 2)
-            advance(Q, 2)
-            receive(p_data, 5, 2)
-            receive(y_data, 6, 3)
-            receive(p_data, 7, 3)
-        if depth > 2:
-            if k == 0:
-                send_sum("dom", slot + 2, wait_sum("panel", slot + 1))
-                interior((K,))
-                advance(K, 3)
-                receive(y_data, 8, 4)
-            for n in range(2, depth):
-                put_operand(y_data, nxt, n, rotate(y_cat, xp_cat, k, n, 1)[0])
-            for n in range(2, depth - 1):
-                put_operand(p_data, nxt, n, rotate(p_cat, pp_cat, k, n, 1)[0])
-        if k > 0:
-            send_sum("dom", slot + 2, wait_sum("panel", slot + 1))
+    scale, ritz = scale_matrices(0, wait_sum("panel", 1))
+    receive(y_data, 4, 2)
+    now = new_y(0, 0, 2)
+    send_sum("panel", 2, node_sums(now[0], now[1]))
+    put_y(0, 0, now)
+    interior((K, Q))
+    advance(K, 2)
+    scale_direction_matrices(scale, ritz)
+    put_p(0, 0, new_p(0, 0, 2))
+    send_sum("dom", 3, wait_sum("panel", 2))
+    advance(Q, 2)
+    interior((K,))
+    receive(p_data, 5, 2)
+    receive(y_data, 6, 3)
+    put_y(0, 2, new_y(0, 2, 1))
+    put_p(0, 2, new_p(0, 2, 1))
+
+    scale, ritz = scale_matrices(1, wait_sum("dom", 3))
+    now = new_y(1, 0, 2)
+    send_sum("panel", 4, node_sums(now[0], now[1]))
+    put_y(1, 0, now)
+    advance(K, 3)
+    scale_direction_matrices(scale, ritz)
+    put_p(1, 0, new_p(1, 0, 2))
+    send_sum("dom", 5, wait_sum("panel", 4))
+    receive(p_data, 7, 3)
+    receive(y_data, 8, 4)
+    put_y(0, 3, new_y(0, 3, 1))
+    put_y(1, 2, new_y(1, 2, 1))
+
+    scale, ritz = scale_matrices(2, wait_sum("dom", 5))
+    now = new_y(2, 0, 2)
+    send_sum("panel", 6, node_sums(now[0], now[1]))
+    put_y(2, 0, now)
+    scale_direction_matrices(scale, ritz)
+    put_p(2, 0, new_p(2, 0, 1))
+    send_sum("dom", 7, wait_sum("panel", 6))
+
+    scale, ritz = scale_matrices(3, wait_sum("dom", 7))
+    now = new_y(3, 0, 1)[0]
+    send_sum("panel", 8, node_sums(now, now))
+    pack(f_block, now)
+    move(f_block)
+    scale_direction_matrices(scale, ritz)
+    pack(f_dirs, new_p(3, 0, 1)[0])
+    move(f_dirs)
+    send_sum("dom", 9, wait_sum("panel", 8))
+
+    for slot in range(2 * ITERS - 1):
+        arrive(far_in[slot].at[pl.ds(0, (n_dom - 1) * halves)], far_send.at[slot])
+    for slot in range(2 * ITERS + 3):
+        arrive(move_in.at[slot, pl.ds(0, n_panel - 1)], move_send.at[slot])
+    for slot in range(2 * ITERS + 2):
+        n = n_panel if slot in (1, 2, 4, 6, 8) else n_dom
+        arrive(sum_in.at[slot, pl.ds(0, n - 1)], sum_send.at[slot])
 
     ritz_column = to_column(ritz + SHIFT)
     narrow = lax.broadcasted_iota(jnp.int32, (width, LANES), 1) == lax.broadcasted_iota(
@@ -498,23 +545,10 @@
 
     assemble(f_block, put_block)
 
-    def drain(out, sem, n, whole):
-        def step(slot, _):
-            if whole:
-                for _ in range(n - 1):
-                    arrive(out.at[slot], sem.at[slot])
-            else:
-                arrive(out.at[slot, pl.ds(0, n - 1)], sem.at[slot])
-            return 0
-
-        lax.fori_loop(0, out.shape[0], step, 0)
-
-    drain(far_out, far_send, n_dom, True)
-    drain(move_out, move_send, n_panel, False)
-    for slot in range(2 * ITERS + 2):
-        n = n_panel if slot in (1, 2, 4, 6, 8) else n_dom
-        for _ in range(n - 1):
-            arrive(sum_out.at[slot], sum_send.at[slot])
+def publish(block_in, dirs_in, ritz_in, block_ref, dirs_ref, ritz_ref, sems):
+    block_ref[...] = block_in[...]
+    dirs_ref[...] = dirs_in[...]
+    ritz_ref[...] = ritz_in[:, : ritz_ref.shape[1]]
 
 
 def local(n_dom, n_panel, *args):
@@ -549,7 +583,7 @@
         vmem((n_bound, LANES, 2 * LANES), bf16),
         vmem((rows, 2 * rows), bf16),
         vmem((rows, 2 * rows), bf16),
-        vmem((rows, 4 * rows), bf16),
+        vmem((2, rows, 4 * rows), bf16),
         vmem((rows, 4 * rows), bf16),
         vmem((2, blocks, width, LANES), f32),
         vmem((blocks, 4 * width, 2 * LANES), bf16),
@@ -593,7 +627,20 @@
         bcols,
         *args[11:],
     )
-    return block, dirs, ritz[0, :width]
+    block, dirs, ritz = pl.pallas_call(
+        publish,
+        out_shape=(
+            jax.ShapeDtypeStruct((width, ndev), f32),
+            jax.ShapeDtypeStruct((width, ndev), f32),
+            jax.ShapeDtypeStruct((1, width), f32),
+        ),
+        in_specs=[pl.BlockSpec(memory_space=pltpu.VMEM)] * 2
+        + [pl.BlockSpec(memory_space=pltpu.VMEM)],
+        out_specs=[pl.BlockSpec(memory_space=pltpu.VMEM)] * 2
+        + [pl.BlockSpec(memory_space=pltpu.VMEM)],
+        scratch_shapes=[dma((2,))],
+    )(block, dirs, ritz)
+    return block, dirs, ritz.reshape(-1)
 
 
 def solution(mesh):

time: 89.1 us -> 74.5 us (0.84)
  Pallas kernels: 83.5 us -> 72.9 us
  local copies, waits for them, and re-layouts: 4.12 us -> 0 us
    pallas_call x1, Pallas kernels: 83.5 us -> 71.3 us  [local(): pl.pallas_call(functools.partial(kernel, ndev * n_dom), out_shape=(jax.Sh...]
    unnamed x2 -> x0, local copies, waits for them, and re-layouts: 2.95 us -> none
    pallas_call x0 -> x1, Pallas kernels: none -> 1.55 us  [local(): pl.pallas_call(publish, out_shape=(jax.ShapeDtypeStruct((width, ndev), f3...]
    squeeze x1 -> x0, local copies, waits for them, and re-layouts: 1.18 us -> none  [local(): return (block, dirs, ritz[0, :width])]
where the time goes in v3:
time: 74.5 us; the launch traced here: 74.3 us
  Pallas kernels  72.9 us (98%)
  between operations  1.45 us (2%)
    pallas_call x1, Pallas kernels, local(): pl.pallas_call(functools.partial(kernel, ndev * n_dom), out_shape=(jax.Sh...  71.3 us
    pallas_call x1, Pallas kernels, local(): pl.pallas_call(publish, out_shape=(jax.ShapeDtypeStruct((width, ndev), f3...  1.55 us

profile of v3, /device:TPU:1, one launch (start us, length us, event | category | flops | bytes accessed | tf_op | source)
XLA Modules:
  0.0 74.3 jit_solution(7662590442715878999)
XLA Ops:
  1.3 71.3 %shard_map.175 = (f32[16,1024]{1,0:T(8,128)}, f32[16,1024]{1,0:T(8,128)}, f32[1,128]{1,0:T(1,128)}) custom-call(f32[16,1024]{1,0:T(8,128)} %start_hbm.1, f32[16,1024]{1,0:T(8,128)} %prior_hbm.1, f32[1,1024]{1,0:T(1,128)} %bitcast.3, f32[32,128,128]{2,1,0:T(8,128)} %tiles_hbm.1, s32[32]{0:T(128)} %trows_hbm.1, s32[32]{0:T(128)} %tcols_hbm.1, ...), custom_call_target="tpu_custom_call" | custom-call | tf_op jit(solution)/shard_map/pallas_call | solution.py:603
  72.6 1.6 %shard_map.176 = (f32[16,1024]{1,0:T(8,128)}, f32[16,1024]{1,0:T(8,128)}, f32[1,16]{1,0:T(1,128)}) custom-call(f32[16,1024]{1,0:T(8,128)} %get-tuple-element.9.block_in, f32[16,1024]{1,0:T(8,128)} %get-tuple-element.10.dirs_in, f32[1,128]{1,0:T(1,128)} %get-tuple-element.11.ritz_in), custom_call_target="tpu_custom_call" | custom-call | tf_op jit(solution)/shard_map/pallas_call | solution.py:630

commit v4 on v3

--- a/solution.py
+++ b/solution.py
@@ -325,8 +325,8 @@
         put_matrix(p_cat, 0, -pr_scaled * ritz)
         put_matrix(p_cat, 1, pr_scaled)
 
-    def new_y(k, first, count):
-        return rotate(y_cat.at[k % 2], xp_cat, k, first, count)
+    def new_y(k, first, count, base=None):
+        return rotate(y_cat.at[k % 2], xp_cat, k, first, count, base)
 
     def new_p(k, first, count):
         return rotate(p_cat, pp_cat, k, first, count)
@@ -339,12 +339,15 @@
         for n, value in enumerate(values):
             put_operand(p_data, (k + 1) % 2, first + n, value)
 
-    def rotate(matrices, from_cat, k, first, count):
+    def from_directions(from_cat, k, first, count):
+        return dot(from_cat[...], p_data[k % 2, :, first * LANES : (first + count) * LANES])
+
+    def rotate(matrices, from_cat, k, first, count, base=None):
         now = k % 2
         lo, hi = first * LANES, (first + count) * LANES
-        total = dot(matrices[:, : 2 * rows], y_data[now, :, lo:hi])
+        total = from_directions(from_cat, k, first, count) if base is None else base
+        total += dot(matrices[:, : 2 * rows], y_data[now, :, lo:hi])
         total += dot(matrices[:, 2 * rows :], y_data[now, :, lo + LANES : hi + LANES])
-        total += dot(from_cat[...], p_data[now, :, lo:hi])
         values = []
         for n in range(count):
             part = total[:, n * LANES : (n + 1) * LANES]
@@ -427,20 +430,22 @@
 
     def advance(kind, j):
         images = boundary(kind, j)
-        square = jnp.zeros((width, LANES), f32)
-        cross = jnp.zeros((width, LANES), f32)
+        if j > 0:
+            send_nodes(2 * (j + 1) + kind, lambda b: images[b])
         if kind == K and j == 0:
+            square = jnp.zeros((width, LANES), f32)
+            cross = jnp.zeros((width, LANES), f32)
             for b in range(blocks):
                 square += field[K, b] * field[K, b]
                 cross += field[K, b] * images[b]
+            send_sum("dom", 0, jnp.concatenate([to_row(square), to_row(cross)], axis=0))
         for b in range(blocks):
             set_block(kind, b, images[b])
         if j + 1 < ITERS - kind:
             choose(kind, j + 1)
             send_far(kind, j + 1)
-        if kind == K and j == 0:
-            send_sum("dom", 0, jnp.concatenate([to_row(square), to_row(cross)], axis=0))
-        send_nodes(2 * (j + 1) + kind, lambda b: field[kind, b])
+        if j == 0:
+            send_nodes(2 * (j + 1) + kind, lambda b: images[b])
 
     f_block, f_dirs = 2 * ITERS + 1, 2 * ITERS + 2
 
@@ -465,14 +470,18 @@
     advance(Q, 0)
     interior((K, Q))
     send_sum("panel", 1, wait_sum("dom", 0))
+    advance(K, 1)
     receive(y_data, 2, 1)
     receive(p_data, 3, 1)
-    advance(K, 1)
     advance(Q, 1)
 
+    base = from_directions(xp_cat, 0, 0, 2)
     scale, ritz = scale_matrices(0, wait_sum("panel", 1))
+    base += dot(y_cat[0, :, : 2 * rows], y_data[0, :, : 2 * LANES])
+    near = base[:, :LANES] + dot(y_cat[0, :, 2 * rows :], y_data[0, :, LANES : 2 * LANES])
     receive(y_data, 4, 2)
-    now = new_y(0, 0, 2)
+    next_ = base[:, LANES:] + dot(y_cat[0, :, 2 * rows :], y_data[0, :, 2 * LANES : 3 * LANES])
+    now = [near + swap(near), next_ + swap(next_)]
     send_sum("panel", 2, node_sums(now[0], now[1]))
     put_y(0, 0, now)
     interior((K, Q))
@@ -487,8 +496,9 @@
     put_y(0, 2, new_y(0, 2, 1))
     put_p(0, 2, new_p(0, 2, 1))
 
+    base = from_directions(xp_cat, 1, 0, 2)
     scale, ritz = scale_matrices(1, wait_sum("dom", 3))
-    now = new_y(1, 0, 2)
+    now = new_y(1, 0, 2, base)
     send_sum("panel", 4, node_sums(now[0], now[1]))
     put_y(1, 0, now)
     advance(K, 3)
@@ -500,16 +510,18 @@
     put_y(0, 3, new_y(0, 3, 1))
     put_y(1, 2, new_y(1, 2, 1))
 
+    base = from_directions(xp_cat, 2, 0, 2)
     scale, ritz = scale_matrices(2, wait_sum("dom", 5))
-    now = new_y(2, 0, 2)
+    now = new_y(2, 0, 2, base)
     send_sum("panel", 6, node_sums(now[0], now[1]))
     put_y(2, 0, now)
     scale_direction_matrices(scale, ritz)
     put_p(2, 0, new_p(2, 0, 1))
     send_sum("dom", 7, wait_sum("panel", 6))
 
+    base = from_directions(xp_cat, 3, 0, 1)
     scale, ritz = scale_matrices(3, wait_sum("dom", 7))
-    now = new_y(3, 0, 1)[0]
+    now = new_y(3, 0, 1, base)[0]
     send_sum("panel", 8, node_sums(now, now))
     pack(f_block, now)
     move(f_block)

time: 74.5 us -> 73.5 us (0.987)
  Pallas kernels: 72.9 us -> 71.9 us
    pallas_call x1, Pallas kernels: 71.3 us -> 70.4 us  [local(): pl.pallas_call(functools.partial(kernel, ndev * n_dom), out_shape=(jax.Sh...]
where the time goes in v4:
time: 73.5 us; the launch traced here: 73.4 us
  Pallas kernels  71.9 us (98%)
  between operations  1.45 us (2%)
    pallas_call x1, Pallas kernels, local(): pl.pallas_call(functools.partial(kernel, ndev * n_dom), out_shape=(jax.Sh...  70.4 us
    pallas_call x1, Pallas kernels, local(): pl.pallas_call(publish, out_shape=(jax.ShapeDtypeStruct((width, ndev), f3...  1.55 us

profile of v4, /device:TPU:1, one launch (start us, length us, event | category | flops | bytes accessed | tf_op | source)
XLA Modules:
  0.0 73.4 jit_solution(7881093731638754270)
XLA Ops:
  1.3 70.4 %shard_map.175 = (f32[16,1024]{1,0:T(8,128)}, f32[16,1024]{1,0:T(8,128)}, f32[1,128]{1,0:T(1,128)}) custom-call(f32[16,1024]{1,0:T(8,128)} %start_hbm.1, f32[16,1024]{1,0:T(8,128)} %prior_hbm.1, f32[1,1024]{1,0:T(1,128)} %bitcast.3, f32[32,128,128]{2,1,0:T(8,128)} %tiles_hbm.1, s32[32]{0:T(128)} %trows_hbm.1, s32[32]{0:T(128)} %tcols_hbm.1, ...), custom_call_target="tpu_custom_call" | custom-call | tf_op jit(solution)/shard_map/pallas_call | solution.py:615
  71.7 1.6 %shard_map.176 = (f32[16,1024]{1,0:T(8,128)}, f32[16,1024]{1,0:T(8,128)}, f32[1,16]{1,0:T(1,128)}) custom-call(f32[16,1024]{1,0:T(8,128)} %get-tuple-element.9.block_in, f32[16,1024]{1,0:T(8,128)} %get-tuple-element.10.dirs_in, f32[1,128]{1,0:T(1,128)} %get-tuple-element.11.ritz_in), custom_call_target="tpu_custom_call" | custom-call | tf_op jit(solution)/shard_map/pallas_call | solution.py:642

commit v5 on v4

--- a/solution.py
+++ b/solution.py
@@ -240,7 +240,7 @@
                 t = i * min(UNROLL, n_bound) + u
                 high, low = split(far_in[slot][bcols[t]])
                 both = jnp.concatenate([high, low], axis=0)
-                product = dot_transposed(jnp.concatenate([both, both], axis=1), bweights[t])
+                product = dot(jnp.concatenate([both, both], axis=1), bweights[t])
                 products.append(product[:width] + product[width:])
                 row_ids.append(brows[t])
             return collect(totals, products, row_ids)
@@ -404,7 +404,7 @@
     got_cuts.wait()
     got_count.wait()
     cut = jnp.where(
-        lax.broadcasted_iota(jnp.int32, (1, n_cut), 1) < count[0], cuts_ref[...], -1
+        lax.broadcasted_iota(jnp.int32, (1, n_cut), 1) < count[...], cuts_ref[...], -1
     )
     for b in range(blocks):
         row = lax.broadcasted_iota(jnp.int32, (LANES, n_cut), 0) + b * LANES
@@ -420,6 +420,14 @@
     choose(Q, 0)
     pl.semaphore_wait(barrier, n_dom + n_panel - 2)
 
+    def split_turned(source, target):
+        def step(t, _):
+            high, low = split(source[t].T)
+            target[t] = jnp.concatenate([high, low], axis=0)
+            return 0
+
+        lax.fori_loop(0, source.shape[0], step, 0)
+
     def split_tiles(source, target):
         def step(t, _):
             high, low = split(source[t])
@@ -433,12 +441,10 @@
         if j > 0:
             send_nodes(2 * (j + 1) + kind, lambda b: images[b])
         if kind == K and j == 0:
-            square = jnp.zeros((width, LANES), f32)
             cross = jnp.zeros((width, LANES), f32)
             for b in range(blocks):
-                square += field[K, b] * field[K, b]
                 cross += field[K, b] * images[b]
-            send_sum("dom", 0, jnp.concatenate([to_row(square), to_row(cross)], axis=0))
+            send_sum("dom", 0, jnp.concatenate([square_row, to_row(cross)], axis=0))
         for b in range(blocks):
             set_block(kind, b, images[b])
         if j + 1 < ITERS - kind:
@@ -450,27 +456,31 @@
     f_block, f_dirs = 2 * ITERS + 1, 2 * ITERS + 2
 
     send_far(K, 0)
-    send_nodes(0, lambda b: field[K, b])
     got_tiles.wait()
     split_tiles(tiles_ref, weights)
     send_far(Q, 0)
-    send_nodes(1, lambda b: field[Q, b])
     got_btiles.wait()
-    split_tiles(btiles_ref, bweights)
+    split_turned(btiles_ref, bweights)
     for copy in got_index:
         copy.wait()
     interior((K, Q))
+    send_nodes(0, lambda b: field[K, b])
+    send_nodes(1, lambda b: field[Q, b])
+    square = jnp.zeros((width, LANES), f32)
+    for b in range(blocks):
+        square += field[K, b] * field[K, b]
+    square_row = to_row(square)
     advance(K, 0)
+    advance(Q, 0)
+    interior((K, Q))
+    send_sum("panel", 1, wait_sum("dom", 0))
+    advance(K, 1)
     for copy in got_rot:
         copy.wait()
     put_matrix(xp_cat, 0, rot_ref[2])
     put_matrix(pp_cat, 0, rot_ref[4])
     receive(y_data, 0, 0)
     receive(p_data, 1, 0)
-    advance(Q, 0)
-    interior((K, Q))
-    send_sum("panel", 1, wait_sum("dom", 0))
-    advance(K, 1)
     receive(y_data, 2, 1)
     receive(p_data, 3, 1)
     advance(Q, 1)
@@ -549,13 +559,15 @@
 
     wait_move(f_dirs)
     assemble(f_dirs, put_dirs)
+    def put_field(b, value):
+        field[K, b] = value
+
     wait_move(f_block)
+    assemble(f_block, put_field)
     scale = to_column(inverse_factor(wait_sum("dom", 2 * ITERS + 1)))
-
-    def put_block(b, value):
-        block_ref[:, b * LANES : (b + 1) * LANES] = value * scale
-
-    assemble(f_block, put_block)
+    for b in range(blocks):
+        block_ref[:, b * LANES : (b + 1) * LANES] = field[K, b] * scale
+
 
 def publish(block_in, dirs_in, ritz_in, block_ref, dirs_ref, ritz_ref, sems):
     block_ref[...] = block_in[...]
@@ -584,7 +596,7 @@
         smem(trows.shape),
         smem(tcols.shape),
         vmem((1, n_cut), i32),
-        smem(count.shape),
+        vmem((1, 1), i32),
         vmem(btiles.shape, f32),
         smem(brows.shape),
         smem(bcols.shape),
@@ -592,7 +604,7 @@
         dma((16,)),
         vmem((ndev, n_cut), bf16),
         vmem((n_tiles, LANES, 2 * LANES), bf16),
-        vmem((n_bound, LANES, 2 * LANES), bf16),
+        vmem((n_bound, 2 * LANES, LANES), bf16),
         vmem((rows, 2 * rows), bf16),
         vmem((rows, 2 * rows), bf16),
         vmem((2, rows, 4 * rows), bf16),
@@ -633,7 +645,7 @@
         trows,
         tcols,
         cuts.reshape(1, -1),
-        count,
+        count.reshape(1, 1),
         btiles,
         brows,
         bcols,

time: 73.5 us -> 72.9 us (level)
  no operation moved by 1% of the time
where the time goes in v5:
time: 72.9 us; the launch traced here: 72.8 us
  Pallas kernels  71.4 us (98%)
  between operations  1.45 us (2%)
    pallas_call x1, Pallas kernels, local(): pl.pallas_call(functools.partial(kernel, ndev * n_dom), out_shape=(jax.Sh...  69.8 us
    pallas_call x1, Pallas kernels, local(): pl.pallas_call(publish, out_shape=(jax.ShapeDtypeStruct((width, ndev), f3...  1.55 us

profile of v5, /device:TPU:1, one launch (start us, length us, event | category | flops | bytes accessed | tf_op | source)
XLA Modules:
  0.0 72.8 jit_solution(16884181611073844070)
XLA Ops:
  1.3 69.8 %shard_map.175 = (f32[16,1024]{1,0:T(8,128)}, f32[16,1024]{1,0:T(8,128)}, f32[1,128]{1,0:T(1,128)}) custom-call(f32[16,1024]{1,0:T(8,128)} %start_hbm.1, f32[16,1024]{1,0:T(8,128)} %prior_hbm.1, f32[1,1024]{1,0:T(1,128)} %bitcast.5, f32[32,128,128]{2,1,0:T(8,128)} %tiles_hbm.1, s32[32]{0:T(128)} %trows_hbm.1, s32[32]{0:T(128)} %tcols_hbm.1, ...), custom_call_target="tpu_custom_call" | custom-call | tf_op jit(solution)/shard_map/pallas_call | solution.py:627
  71.1 1.6 %shard_map.176 = (f32[16,1024]{1,0:T(8,128)}, f32[16,1024]{1,0:T(8,128)}, f32[1,16]{1,0:T(1,128)}) custom-call(f32[16,1024]{1,0:T(8,128)} %get-tuple-element.9.block_in, f32[16,1024]{1,0:T(8,128)} %get-tuple-element.10.dirs_in, f32[1,128]{1,0:T(1,128)} %get-tuple-element.11.ritz_in), custom_call_target="tpu_custom_call" | custom-call | tf_op jit(solution)/shard_map/pallas_call | solution.py:654

commit v6 on v5

--- a/solution.py
+++ b/solution.py
@@ -483,12 +483,12 @@
     receive(p_data, 1, 0)
     receive(y_data, 2, 1)
     receive(p_data, 3, 1)
-    advance(Q, 1)
 
     base = from_directions(xp_cat, 0, 0, 2)
     scale, ritz = scale_matrices(0, wait_sum("panel", 1))
     base += dot(y_cat[0, :, : 2 * rows], y_data[0, :, : 2 * LANES])
     near = base[:, :LANES] + dot(y_cat[0, :, 2 * rows :], y_data[0, :, LANES : 2 * LANES])
+    advance(Q, 1)
     receive(y_data, 4, 2)
     next_ = base[:, LANES:] + dot(y_cat[0, :, 2 * rows :], y_data[0, :, 2 * LANES : 3 * LANES])
     now = [near + swap(near), next_ + swap(next_)]

time: 72.9 us -> 73 us (level)
  no operation moved by 1% of the time
where the time goes in v6:
time: 73 us; the launch traced here: 72.9 us
  Pallas kernels  71.4 us (98%)
  between operations  1.45 us (2%)
    pallas_call x1, Pallas kernels, local(): pl.pallas_call(functools.partial(kernel, ndev * n_dom), out_shape=(jax.Sh...  69.9 us
    pallas_call x1, Pallas kernels, local(): pl.pallas_call(publish, out_shape=(jax.ShapeDtypeStruct((width, ndev), f3...  1.55 us

profile of v6, /device:TPU:1, one launch (start us, length us, event | category | flops | bytes accessed | tf_op | source)
XLA Modules:
  0.0 72.9 jit_solution(12977882854196637870)
XLA Ops:
  1.3 69.9 %shard_map.175 = (f32[16,1024]{1,0:T(8,128)}, f32[16,1024]{1,0:T(8,128)}, f32[1,128]{1,0:T(1,128)}) custom-call(f32[16,1024]{1,0:T(8,128)} %start_hbm.1, f32[16,1024]{1,0:T(8,128)} %prior_hbm.1, f32[1,1024]{1,0:T(1,128)} %bitcast.5, f32[32,128,128]{2,1,0:T(8,128)} %tiles_hbm.1, s32[32]{0:T(128)} %trows_hbm.1, s32[32]{0:T(128)} %tcols_hbm.1, ...), custom_call_target="tpu_custom_call" | custom-call | tf_op jit(solution)/shard_map/pallas_call | solution.py:627
  71.1 1.6 %shard_map.176 = (f32[16,1024]{1,0:T(8,128)}, f32[16,1024]{1,0:T(8,128)}, f32[1,16]{1,0:T(1,128)}) custom-call(f32[16,1024]{1,0:T(8,128)} %get-tuple-element.9.block_in, f32[16,1024]{1,0:T(8,128)} %get-tuple-element.10.dirs_in, f32[1,128]{1,0:T(1,128)} %get-tuple-element.11.ritz_in), custom_call_target="tpu_custom_call" | custom-call | tf_op jit(solution)/shard_map/pallas_call | solution.py:654
